TPU v7x, 128 devices: a whole 4x4x4 slice. The times are simulated.
128 devices in a mesh: expert: 16 (over x, z_lo, core), dp: 8 (over y, z_hi).
Axes of the slice: x: 4, y: 4, z: 4 (z_hi: 2, z_lo: 2; z = z_hi * 2 + z_lo), core: 2. Of those that a mesh axis runs over, the one named last changes fastest.
Arguments:
- tokens: bfloat16 [16384, 2048], P(('expert', 'dp')), may hold values from -6 to 6
- cotangent: bfloat16 [16384, 2048], P(('expert', 'dp')), may hold values from -1.5 to 1.5
- route_gates: float32 [16384, 6], P(('expert', 'dp')), may hold values from 0.1 to 1
- expert_ids: int32 [16384, 6], P(('expert', 'dp')), may hold values from 0 to 31, as said below
- slot_index: int32 [16384, 6], P(('expert', 'dp')), may hold values from 0 to 31, as said below
- w_gate: bfloat16 [32, 2048, 704], P('expert'), may hold values from -0.125 to 0.125
- w_up: bfloat16 [32, 2048, 704], P('expert'), may hold values from -0.125 to 0.125
- w_down: bfloat16 [32, 704, 2048], P('expert'), may hold values from -0.21875 to 0.21875
Outputs:
- layer_out: bfloat16 [16384, 2048], P(('expert', 'dp'))
- grad_tokens: bfloat16 [16384, 2048], P(('expert', 'dp'))
- grad_gates: float32 [16384, 6], P(('expert', 'dp'))
- grad_w_gate: float32 [32, 2048, 704], P('expert', 'dp')
- grad_w_up: float32 [32, 2048, 704], P('expert', 'dp')
- grad_w_down: float32 [32, 704, 2048], P('expert', None, 'dp')
Inputs may be any that keep to these rules, and one draw needn't show every extreme that they name: `expert_ids`: each row names 6 different experts. Among the rows of one device no expert is named more than 32 times, and in the rows of every device some expert is named exactly 32 times. `slot_index`: among the rows of one device, the choices that name the same expert have distinct slots.
All inputs are finite; a program needn't handle non-finite values.
Results may differ from a plain program's by a relative error of at most 0.014.
Values may be sent and summed in bfloat16 or wider, within the bound.
A program may use at most 192 MiB of HBM per device.

v0:
```python
import functools

import jax
import jax.numpy as jnp
from jax import lax
from jax.experimental import pallas as pl
from jax.experimental.pallas import tpu as pltpu
from jax.sharding import PartitionSpec as P

MESH = pl.DeviceIdType.MESH
F32 = jnp.float32
BF16 = jnp.bfloat16
NX = 4
NY = 4
H_ROWS = 704
W_COLS = 256


def slot_of(dx, dz, dc):
    return (dx % NX) * 4 + (dz % 2) * 2 + (dc % 2)


class Place:
    def __init__(self):
        e = lax.axis_index("expert")
        q = lax.axis_index("dp")
        self.e, self.q = e, q
        self.x, self.zl, self.c = e // 4, (e // 2) % 2, e % 2
        self.y, self.zh = q // 2, q % 2

    def group(self, dx=0, dz=0, dc=0):
        x = lax.rem(self.x + (dx % NX), NX) if dx % NX else self.x
        z = 1 - self.zl if dz % 2 else self.zl
        c = 1 - self.c if dc % 2 else self.c
        return (x * 4 + z * 2 + c, self.q)

    def col(self, dy=0, dz=0):
        y = lax.rem(self.y + (dy % NY), NY) if dy % NY else self.y
        z = 1 - self.zh if dz % 2 else self.zh
        return (self.e, y * 2 + z)


def enter(peers):
    barrier = pltpu.get_barrier_semaphore()
    for peer in peers:
        pl.semaphore_signal(barrier, inc=1, device_id=peer, device_id_type=MESH)
    pl.semaphore_wait(barrier, len(peers))


class Sends:
    def __init__(self, send_sem, recv_sem):
        self.send_sem, self.recv_sem = send_sem, recv_sem
        self.made = []

    def start(self, src, dst, peer):
        i = len(self.made)
        copy = pltpu.make_async_remote_copy(
            src_ref=src,
            dst_ref=dst,
            send_sem=self.send_sem.at[i],
            recv_sem=self.recv_sem.at[i],
            device_id=peer,
            device_id_type=MESH,
        )
        copy.start()
        self.made.append(copy)
        return copy

    def drain(self):
        for copy in self.made:
            copy.wait_send()


GROUP = [(dx, dz, dc) for dx in range(NX) for dz in range(2) for dc in range(2)]
A = (0, 64)
B = (64, 128)
A0, A1, B0, B1 = (0, 32), (32, 64), (64, 96), (96, 128)


def gather_rows(sends, place, own, buf):
    arrived = {}

    def push(dx, dz, dc, rows, ddx=0, ddz=0, ddc=0):
        lo, hi = rows
        here = own if (dx, dz, dc) == (0, 0, 0) else buf.at[slot_of(dx, dz, dc)]
        there = ((dx - ddx) % NX, (dz - ddz) % 2, (dc - ddc) % 2)
        arrived[there + (rows,)] = sends.start(
            here.at[pl.ds(lo, hi - lo)],
            buf.at[slot_of(*there), pl.ds(lo, hi - lo)],
            place.group(ddx, ddz, ddc),
        )

    def take(dx, dz, rows):
        arrived[(dx % NX, dz % 2, 0, rows)].wait_recv()
        push(dx % NX, dz % 2, 0, rows, ddc=1)

    yield
    push(0, 0, 0, B, ddz=1)
    push(0, 0, 0, A, ddx=1)
    push(0, 0, 0, A, ddx=-1)
    push(0, 0, 0, B, ddx=1)
    push(0, 0, 0, B, ddx=-1)
    push(0, 0, 0, A, ddz=1)
    push(0, 0, 0, (0, 128), ddc=1)
    yield
    take(0, 1, B)
    push(0, 1, 0, B, ddx=1)
    push(0, 1, 0, B, ddx=-1)
    yield
    take(1, 0, A)
    push(1, 0, 0, A0, ddx=-1)
    push(1, 0, 0, A, ddz=1)
    take(-1, 0, A)
    push(3, 0, 0, A1, ddx=1)
    push(3, 0, 0, A, ddz=1)
    yield
    take(1, 0, B)
    push(1, 0, 0, B0, ddx=-1)
    take(-1, 0, B)
    push(3, 0, 0, B1, ddx=1)
    take(0, 1, A)
    yield
    take(1, 1, B)
    push(1, 1, 0, B0, ddx=-1)
    take(-1, 1, B)
    push(3, 1, 0, B1, ddx=1)
    take(2, 0, A0)
    push(2, 0, 0, A0, ddz=1)
    take(2, 0, A1)
    push(2, 0, 0, A1, ddz=1)
    yield
    take(1, 1, A)
    take(3, 1, A)
    take(2, 0, B0)
    take(2, 0, B1)
    take(2, 1, B0)
    take(2, 1, B1)
    take(2, 1, A0)
    take(2, 1, A1)
    yield
    for key in list(arrived):
        if key[2] == 1:
            arrived[key].wait_recv()
    yield


def forward_kernel(
    tok, cot, meta, wg_hbm, wu_hbm, wd_hbm,
    routed_o, dy_o, pre_o, hidden_o, rows_o, gates_o, pick,
    tok_all, cot_all, meta_all, wg, wu, wd, routed, y_rows, dy, pre, hidden, hidden_t, gate_col,
    send_sem, recv_sem, copy_sem,
):
    place = Place()
    enter([place.group(*r) for r in GROUP[1:]])
    copies = []

    def local(src, dst):
        copy = pltpu.make_async_copy(src, dst, copy_sem.at[len(copies)])
        copy.start()
        copies.append(copy)
        return copy

    tok_sends = Sends(send_sem.at[pl.ds(0, 48)], recv_sem.at[pl.ds(0, 48)])
    cot_sends = Sends(send_sem.at[pl.ds(48, 48)], recv_sem.at[pl.ds(48, 48)])
    sends = Sends(send_sem.at[pl.ds(96, 16)], recv_sem.at[pl.ds(96, 16)])
    metas = []
    for r in GROUP[1:]:
        dst = meta_all.at[slot_of(-r[0], r[1], r[2])]
        metas.append(sends.start(meta, dst, place.group(*r)))
    first = gather_rows(tok_sends, place, tok, tok_all)
    second = gather_rows(cot_sends, place, cot, cot_all)
    next(first)
    next(second)
    next(first)
    own = [local(tok, tok_all.at[0]), local(cot, cot_all.at[0]), local(meta, meta_all.at[0])]
    weights = [local(wg_hbm, wg), local(wu_hbm, wu), local(wd_hbm, wd)]
    next(first)
    for copy in metas:
        copy.wait_recv()
    for copy in own:
        copy.wait()
    slot = (lax.broadcasted_iota(jnp.int32, (64, 128), 0) + place.e * 64).astype(F32)

    @pl.loop(0, 16)
    def _(j):
        total = jnp.zeros((64, 128), F32)
        gate = jnp.zeros((64, 128), F32)
        for k in range(6):
            hit = slot == jnp.broadcast_to(meta_all[j, k : k + 1], (64, 128))
            total = total + jnp.where(hit, 1.0, 0.0)
            row = jnp.broadcast_to(meta_all[j, 8 + k : 9 + k], (64, 128))
            gate = gate + jnp.where(hit, row, 0.0)
        pick[j] = total.astype(BF16)
        gate_col[j] = jnp.broadcast_to(jnp.sum(gate, axis=1, keepdims=True), (64, 128))

    next(first)
    next(first)
    next(first)
    next(second)
    for _ in first:
        pass
    next(second)

    def rows32(j):
        return pl.ds(pl.multiple_of(j * 32, 32), 32)

    @pl.loop(0, 16)
    def _(j):
        got = jnp.dot(pick[j], tok_all[j], preferred_element_type=F32).astype(BF16)
        routed[0, rows32(j)] = got[0:32]
        routed[1, rows32(j)] = got[32:64]

    routed_out = local(routed, routed_o)
    next(second)
    for copy in weights:
        copy.wait()

    def up(e):
        pre[e, 0] = jnp.dot(routed[e], wg[e], preferred_element_type=F32)
        pre[e, 1] = jnp.dot(routed[e], wu[e], preferred_element_type=F32)

        @pl.loop(0, 16)
        def _(i):
            at = rows32(i)
            gate = pre[e, 0, at]
            hidden[e, at] = (gate * jax.nn.sigmoid(gate) * pre[e, 1, at]).astype(BF16)

        local(pre.at[e], pre_o.at[e])

    def down(e):
        hidden_t[e] = hidden[e].T
        local(hidden_t.at[e], hidden_o.at[e])
        for n in range(2):
            at = pl.ds(n * 1024, 1024)
            y_rows[e, :, at] = jnp.dot(
                hidden[e], wd[e, :, at], preferred_element_type=F32
            ).astype(BF16)

    up(0)
    next(second)
    up(1)
    next(second)
    down(0)
    next(second)
    down(1)
    tok_sends.drain()

    def both(ref, j):
        return jnp.concatenate([ref[0, rows32(j)], ref[1, rows32(j)]], axis=0)

    @pl.loop(0, 16)
    def _(j):
        scaled = (both(y_rows, j).astype(F32) * gate_col[j, :, 0:1]).astype(BF16)
        tok_all[j] = lax.dot_general(
            pick[j], scaled, (((0,), (0,)), ((), ())), preferred_element_type=F32
        ).astype(BF16)

    local(tok_all, rows_o)
    for _ in second:
        pass

    @pl.loop(0, 16)
    def _(j):
        got = jnp.dot(pick[j], cot_all[j], preferred_element_type=F32)
        by_slot = jnp.sum(got * both(y_rows, j).astype(F32), axis=1, keepdims=True)
        scaled = (got * gate_col[j, :, 0:1]).astype(BF16)
        dy[0, rows32(j)] = scaled[0:32]
        dy[1, rows32(j)] = scaled[32:64]
        by_slot = jnp.broadcast_to(by_slot, (64, 128))
        parts = []
        for k in range(6):
            hit = slot == jnp.broadcast_to(meta_all[j, k : k + 1], (64, 128))
            parts.append(jnp.sum(jnp.where(hit, by_slot, 0.0), axis=0, keepdims=True))
        parts.append(jnp.zeros((2, 128), F32))
        gates_o[j] = jnp.concatenate(parts, axis=0)

    local(dy, dy_o)
    for copy in copies[6:]:
        copy.wait()
    cot_sends.drain()
    sends.drain()


def forward(tok, cot, meta, w_gate, w_up, w_down):
    d = tok.shape[1]
    hbm = pl.BlockSpec(memory_space=pl.ANY)
    vmem = pl.BlockSpec(memory_space=pltpu.VMEM)
    return pl.pallas_call(
        forward_kernel,
        out_shape=(
            jax.ShapeDtypeStruct((2, 512, d), BF16),
            jax.ShapeDtypeStruct((2, 512, d), BF16),
            jax.ShapeDtypeStruct((2, 2, 512, H_ROWS), F32),
            jax.ShapeDtypeStruct((2, H_ROWS, 512), BF16),
            jax.ShapeDtypeStruct((16, 128, d), BF16),
            jax.ShapeDtypeStruct((16, 8, 128), F32),
            jax.ShapeDtypeStruct((16, 64, 128), BF16),
        ),
        in_specs=[hbm] * 6,
        out_specs=(hbm, hbm, hbm, hbm, hbm, vmem, vmem),
        scratch_shapes=[
            pltpu.VMEM((16, 128, d), BF16),
            pltpu.VMEM((16, 128, d), BF16),
            pltpu.VMEM((16,) + meta.shape, F32),
            pltpu.VMEM(w_gate.shape, BF16),
            pltpu.VMEM(w_up.shape, BF16),
            pltpu.VMEM(w_down.shape, BF16),
            pltpu.VMEM((2, 512, d), BF16),
            pltpu.VMEM((2, 512, d), BF16),
            pltpu.VMEM((2, 512, d), BF16),
            pltpu.VMEM((2, 2, 512, H_ROWS), F32),
            pltpu.VMEM((2, 512, H_ROWS), BF16),
            pltpu.VMEM((2, H_ROWS, 512), BF16),
            pltpu.VMEM((16, 64, 128), F32),
            pltpu.SemaphoreType.DMA((112,)),
            pltpu.SemaphoreType.DMA((112,)),
            pltpu.SemaphoreType.DMA((16,)),
        ],
        compiler_params=pltpu.CompilerParams(
            collective_id=0, has_side_effects=True, vmem_limit_bytes=62 * 2**20
        ),
    )(tok, cot, meta, w_gate, w_up, w_down)


def add_into(dst, terms, chunk):
    rows = dst.shape[0]

    @pl.loop(0, rows // chunk)
    def _(i):
        at = pl.ds(pl.multiple_of(i * chunk, chunk), chunk)
        total = terms[0][at].astype(F32)
        for term in terms[1:]:
            total = total + term[at].astype(F32)
        dst[at] = total.astype(dst.dtype)


class Tree:
    def __init__(self, sends, peer, part, land, out, chunk):
        self.sends, self.peer, self.part = sends, peer, part
        self.land, self.out, self.chunk = land, out, chunk

    def open(self):
        s, p, peer = self.sends, self.part, self.peer
        self.far = [
            s.start(p(2, 0), self.land(0, 0), peer(-1)),
            s.start(p(2, 1), self.land(0, 1), peer(1)),
        ]
        self.near = [
            s.start(p(1, 0), self.land(1, 0), peer(1)),
            s.start(p(-1, 1), self.land(1, 1), peer(-1)),
        ]

    def relay(self):
        self.via = []
        for h, d in ((0, -1), (1, 1)):
            self.far[h].wait_recv()
            add_into(self.out(h), [self.part(d, h), self.land(0, h)], self.chunk)
            self.via.append(self.sends.start(self.out(h), self.land(2, h), self.peer(d)))

    def close(self, h):
        self.near[h].wait_recv()
        self.via[h].wait_recv()
        return [self.part(0, h), self.land(1, h), self.land(2, h)]


def reduce_kernel(
    p_gate, p_up, p_down, o_first, o_second, gates_in,
    out_first, out_second, gates_out, grads_out,
    own_p, land_y, land_z, out_y, out_z, t_down, land_d, land_dz, out_d,
    t_rows, land_s, land_xb, out_xb, v_rows, land_zb,
    gates_land, send_sem, recv_sem, load_sem,
):
    place = Place()
    peers = [place.group(*r) for r in GROUP[1:]] + [place.col(1), place.col(-1), place.col(0, 1)]
    enter(peers)
    sends = Sends(send_sem, recv_sem)
    o_hbm = (o_first, o_second)
    p_hbm = (p_gate, p_up, p_down)
    rows_out = (out_first, out_second)
    loads = []

    def load(src, dst):
        copy = pltpu.make_async_copy(src, dst, load_sem.at[len(loads)])
        copy.start()
        loads.append(copy)
        return copy

    def yy(d):
        return lax.rem(place.y + (d % NY), NY) if d % NY else place.y

    def p_slice(m, e, d, z):
        at = pl.multiple_of((yy(d) * 2 + z) * W_COLS, W_COLS)
        return p_hbm[m].at[e, :, pl.ds(at, W_COLS)]

    shares = []
    for r in range(2):
        got = []
        for dx in range(NX):
            for dz in range(2):
                got.append(
                    sends.start(
                        o_hbm[r].at[slot_of(dx, dz, 1)], land_s.at[r, dx * 2 + dz],
                        place.group(0, 0, 1),
                    )
                )
        shares.append(got)
    down_z = {}
    own_loads = {}
    for e in range(2):
        for d in (2, 1, 3, 0):
            down_z[e, d] = sends.start(
                p_slice(2, e, d, 1 - place.zh), land_dz.at[e, d], place.col(0, 1)
            )
    trees = []
    for m in range(2):
        for e in range(2):
            me = m * 2 + e

            def part(d, h, m=m, e=e, me=me):
                return own_part(m, e, me, d, h)

            def own_part(m, e, me, d, h):
                return p_slice(m, e, d, h)

            def held(d, h, me=me):
                return own_p.at[me, {-1: 0, 1: 1, 0: 2 + h}[d]]

            def land(k, h, me=me):
                return land_y.at[me, k, h]

            def out(h, me=me):
                return out_y.at[me, h]

            tree = Tree(sends, place.col, part, land, out, 64)
            tree.open()
            tree.part = held
            own_loads[me] = [
                load(p_slice(m, e, -1, 0), own_p.at[me, 0]),
                load(p_slice(m, e, 1, 1), own_p.at[me, 1]),
                load(p_slice(m, e, 0, 0), own_p.at[me, 2]),
                load(p_slice(m, e, 0, 1), own_p.at[me, 3]),
            ]
            trees.append(tree)
    for e in range(2):
        own_loads[4 + e] = [
            load(p_slice(2, e, d, place.zh), t_down.at[e, d]) for d in range(NY)
        ]
    own_rows = [
        load(o_hbm[r].at[slot_of(dx, dz, 0)], t_rows.at[r, dx * 2 + dz])
        for r in range(2) for dx in range(NX) for dz in range(2)
    ]
    gate_sends = []
    for r in GROUP[1:]:
        gate_sends.append(
            sends.start(
                gates_in.at[slot_of(*r)], gates_land.at[slot_of(-r[0], r[1], r[2])],
                place.group(*r),
            )
        )

    row_state = []
    for r in range(2):
        for i in range(8):
            shares[r][i].wait_recv()
            own_rows[r * 8 + i].wait()
            add_into(t_rows.at[r, i], [t_rows.at[r, i], land_s.at[r, i]], 32)
        trees_x = []
        for dz in (1, 0):
            tree = Tree(
                sends, place.group,
                lambda d, h, r=r, dz=dz: t_rows.at[r, (d % NX) * 2 + dz, pl.ds(64 * h, 64)],
                lambda k, h, r=r, dz=dz: land_xb.at[r, dz, k, h],
                lambda h, r=r, dz=dz: out_xb.at[r, dz, h],
                32,
            )
            tree.open()
            trees_x.append(tree)
        row_state.append(trees_x)

    def rows_mid(r):
        for tree in row_state[r]:
            tree.relay()

    def rows_end(r):
        for h in range(2):
            add_into(v_rows.at[r, 1, pl.ds(64 * h, 64)], row_state[r][0].close(h), 32)
        copy = sends.start(v_rows.at[r, 1], land_zb.at[r], place.group(0, 1, 0))
        for h in range(2):
            add_into(v_rows.at[r, 0, pl.ds(64 * h, 64)], row_state[r][1].close(h), 32)
        return copy

    def rows_last(r, copy):
        copy.wait_recv()
        add_into(rows_out[r], [v_rows.at[r, 0], land_zb.at[r]], 32)

    def down_mid(e):
        for copy in own_loads[4 + e]:
            copy.wait()
        for d in (2, 1, 3, 0):
            down_z[e, d].wait_recv()
            add_into(t_down.at[e, d], [t_down.at[e, d], land_dz.at[e, d]], 64)
        half = H_ROWS // 2
        tree = Tree(
            sends, place.col,
            lambda d, h: t_down.at[e, d % NY, pl.ds(half * h, half)],
            lambda k, h: land_d.at[e, k, pl.ds(half * h, half)],
            lambda h: out_d.at[e, pl.ds(half * h, half)],
            32,
        )
        tree.open()
        return tree

    def down_end(e, tree):
        half = H_ROWS // 2
        for h in range(2):
            add_into(grads_out.at[2, e, pl.ds(half * h, half)], tree.close(h), 32)

    def y_relay(me):
        for copy in own_loads[me]:
            copy.wait()
        trees[me].relay()

    def y_end(me):
        tree = trees[me]
        for h in range(2):
            terms = tree.close(h)

            @pl.when(place.zh != h)
            def _():
                add_into(out_z.at[me], terms, 64)

            @pl.when(place.zh == h)
            def _():
                add_into(grads_out.at[me // 2, me % 2], terms, 64)

        return sends.start(out_z.at[me], land_z.at[me], place.col(0, 1))

    def z_end(me, copy):
        copy.wait_recv()
        dst = grads_out.at[me // 2, me % 2]
        add_into(dst, [dst, land_z.at[me]], 64)

    y_relay(0)
    rows_mid(0)
    y_relay(1)
    d0 = down_mid(0)
    rows_mid(1)
    y_relay(2)
    r0 = rows_end(0)
    d1 = down_mid(1)
    y_relay(3)
    z0 = y_end(0)
    r1 = rows_end(1)
    d0.relay()
    z1 = y_end(1)
    rows_last(0, r0)
    d1.relay()
    z2 = y_end(2)
    rows_last(1, r1)
    z_end(0, z0)
    down_end(0, d0)
    z3 = y_end(3)
    z_end(1, z1)
    down_end(1, d1)
    z_end(2, z2)
    for copy in gate_sends:
        copy.wait_recv()
    total = gates_in[0]
    for i in range(1, 16):
        total = total + gates_land[i]
    gates_out[...] = total
    z_end(3, z3)
    sends.drain()


def reduce_all(p_gate, p_up, p_down, o_first, o_second, gates_in):
    d = o_first.shape[-1]
    n = 192
    hbm = pl.BlockSpec(memory_space=pl.ANY)
    vmem = pl.BlockSpec(memory_space=pltpu.VMEM)
    slab = (H_ROWS, W_COLS)

    def buf(*shape):
        return pltpu.VMEM(shape, BF16)

    return pl.pallas_call(
        reduce_kernel,
        out_shape=(
            jax.ShapeDtypeStruct((128, d), BF16),
            jax.ShapeDtypeStruct((128, d), BF16),
            jax.ShapeDtypeStruct((8, 128), F32),
            jax.ShapeDtypeStruct((3, 2) + slab, F32),
        ),
        in_specs=[hbm] * 5 + [vmem],
        out_specs=(vmem,) * 4,
        scratch_shapes=[
            buf(4, 4, *slab), buf(4, 3, 2, *slab), buf(4, *slab), buf(4, 2, *slab),
            buf(4, *slab), buf(2, 4, *slab), buf(2, 3, *slab), buf(2, 4, *slab), buf(2, *slab),
            buf(2, 8, 128, d), buf(2, 8, 128, d), buf(2, 2, 3, 2, 64, d), buf(2, 2, 2, 64, d),
            buf(2, 2, 128, d), buf(2, 128, d),
            pltpu.VMEM((16, 8, 128), F32),
            pltpu.SemaphoreType.DMA((n,)),
            pltpu.SemaphoreType.DMA((n,)),
            pltpu.SemaphoreType.DMA((64,)),
        ],
        compiler_params=pltpu.CompilerParams(
            collective_id=1, has_side_effects=True, vmem_limit_bytes=62 * 2**20
        ),
    )(p_gate, p_up, p_down, o_first, o_second, gates_in)


def dot(spec, a, b):
    return jnp.einsum(spec, a, b, preferred_element_type=F32)


def shards(tokens, cotangent, route_gates, expert_ids, slot_index, w_gate, w_up, w_down):
    d = tokens.shape[1]
    target = (expert_ids * 32 + slot_index).astype(F32).T
    meta = jnp.zeros((16, 128), F32).at[0:6].set(target).at[8:14].set(route_gates.T)
    routed, grad_rows, pre, hidden_t, o_out, gates_in, pick = forward(
        tokens, cotangent, meta, w_gate, w_up, w_down
    )

    def by_block(v):
        return v.reshape(2, 16, 32, -1).transpose(1, 0, 2, 3).reshape(16, 64, -1)

    gate_pre, up_pre = pre[:, 0], pre[:, 1]
    grad_hidden = dot("ecd,ehd->ech", grad_rows, w_down)
    s = jax.nn.sigmoid(gate_pre)
    d_gate = (grad_hidden * up_pre * s * (1.0 + gate_pre * (1.0 - s))).astype(BF16)
    d_up = (grad_hidden * gate_pre * s).astype(BF16)
    d_in = dot("ech,edh->ecd", d_gate, w_gate) + dot("ech,edh->ecd", d_up, w_up)
    o_grad = dot("bit,bid->btd", pick, by_block(d_in.astype(BF16))).astype(BF16)
    out, grad, gates, grads = reduce_all(
        dot("ech,ecd->ehd", d_gate, routed).astype(BF16),
        dot("ech,ecd->ehd", d_up, routed).astype(BF16),
        dot("ehc,ecd->ehd", hidden_t, grad_rows).astype(BF16),
        o_out, o_grad, gates_in,
    )
    return (
        out,
        grad,
        gates[0:6].T,
        grads[0].transpose(0, 2, 1),
        grads[1].transpose(0, 2, 1),
        grads[2],
    )


def solution(mesh):
    row = P(("expert", "dp"), None)
    weight = P("expert", None, None)
    return jax.shard_map(
        shards,
        mesh=mesh,
        in_specs=(row, row, row, row, row, weight, weight, weight),
        out_specs=(row, row, row, P("expert", "dp", None), P("expert", "dp", None), P("expert", None, "dp")),
        check_vma=False,
    )
```

profile of v0, /device:TPU:1, one launch (start us, length us, event | category | flops | bytes accessed | tf_op | source)
XLA Modules:
  0.0 289.1 jit_solution(15111391124753111752)
XLA Ops:
  0.6 8.5 %copy.24.wg_hbm = bf16[2,2048,704]{2,1,0:T(8,128)(2,1)} copy(bf16[2,2048,704]{1,2,0:T(8,128)(2,1)} %param.17) | data formatting | bytes 11534336 | tf_op args[5]
  9.1 8.6 %copy.25.wu_hbm = bf16[2,2048,704]{2,1,0:T(8,128)(2,1)} copy(bf16[2,2048,704]{1,2,0:T(8,128)(2,1)} %param.18) | data formatting | bytes 11534336 | tf_op args[6]
  17.7 0.0 copy-done.5
  17.7 0.1 scatter.9.meta
  17.8 0.0 copy-start.3
  17.9 0.6 copy-done.3
  18.4 81.7 %shard_map.127 = (bf16[2,512,2048]{2,1,0:T(8,128)(2,1)}, bf16[2,512,2048]{2,1,0:T(8,128)(2,1)}, f32[2,2,512,704]{3,2,1,0:T(8,128)}, bf16[2,704,512]{2,1,0:T(8,12...) custom-call(bf16[128,2048]{1,0:T(8,128)(2,1)} %tok.1, ...), custom_call_target="tpu_custom_call" | custom-call | tf_op jit(solution)/shard_map/pallas_call | solution.py:288
  100.2 0.0 slice-start.1
  100.2 11.3 %fusion.7 = (bf16[2,512,704]{2,1,0:T(8,128)(2,1)S(1)}, bf16[2,512,704]{2,1,0:T(8,128)(2,1)}) fusion(f32[2,2,512,704]{3,2,1,0:T(8,128)} %get-tuple-element.42, bf16[2,512,2048]{2,1,0:T(8,128)(2,1)} %get-tuple-element.41, bf16[2,704,2048]{2,1,0:T(8,128)(2,1)} %wd_hbm.1), kind=kOutput, calls=%fused_computation.15 | convolution fusion | flops 2962161664 | bytes 18612224 | tf_op jit(solution)/shard_map/ecd,ehd->ech/dot_general | solution.py:613
  111.4 0.0 slice-done
  111.4 4.8 %fusion.9 = f32[2,512,2048]{2,1,0:T(8,128)S(1)} fusion(bf16[2,512,704]{2,1,0:T(8,128)(2,1)} %get-tuple-element.53, bf16[2,2048,704]{1,2,0:T(8,128)(2,1)S(1)} %bitcast.65), kind=kOutput, calls=%fused_computation.23 | convolution fusion | flops 2952790016 | bytes 15597568 | tf_op jit(solution)/shard_map/ech,edh->ecd/dot_general | solution.py:613
  116.3 6.3 %add_convert_fusion = bf16[2,512,2048]{2,1,0:T(8,128)(2,1)S(1)} fusion(f32[2,512,2048]{2,1,0:T(8,128)S(1)} %fusion.9, bf16[2,512,704]{2,1,0:T(8,128)(2,1)S(1)} %get-tuple-element.52, bf16[2,2048,704]{1,2,0:T(8,128)(2,1)} %param.18), kind=kOutput, calls=%fused_computation | convolution fusion | flops 2956984320 | bytes 19791872 | tf_op jit(solution)/shard_map/ech,edh->ecd/dot_general | solution.py:613
  122.6 0.0 copy-start.2
  122.6 0.6 copy.32
  123.2 0.4 copy-done.2
  123.5 5.6 %convolution_convert_fusion.o_second = bf16[16,128,2048]{2,1,0:T(8,128)(2,1)} fusion(bf16[16,64,128]{2,1,0:T(8,128)(2,1)S(1)} %copy-done.2, bf16[16,64,2048]{2,1,0:T(8,128)(2,1)S(1)} %bitcast.63), kind=kOutput, calls=%fused_computation.1 | convolution fusion | flops 541065216 | bytes 12845056 | tf_op jit(solution)/shard_map/bit,bid->btd/dot_general | solution.py:613
  129.1 5.0 %convolution_convert_fusion.2.p_up = bf16[2,704,2048]{2,1,0:T(8,128)(2,1)} fusion(bf16[2,512,704]{2,1,0:T(8,128)(2,1)S(1)} %get-tuple-element.52, bf16[2,512,2048]{2,1,0:T(8,128)(2,1)S(1)} %copy-done.9), kind=kOutput, calls=%fused_computation.3 | convolution fusion | flops 2955673600 | bytes 11403264 | tf_op jit(solution)/shard_map/ech,ecd->ehd/dot_general | solution.py:613
  134.2 5.0 %convolution_convert_fusion.3.p_gate = bf16[2,704,2048]{2,1,0:T(8,128)(2,1)} fusion(bf16[2,512,704]{2,1,0:T(8,128)(2,1)S(1)} %copy-done.11, bf16[2,512,2048]{2,1,0:T(8,128)(2,1)S(1)} %copy-done.9), kind=kOutput, calls=%fused_computation.4 | convolution fusion | flops 2955673600 | bytes 11403264 | tf_op jit(solution)/shard_map/ech,ecd->ehd/dot_general | solution.py:613
  139.2 4.9 %convolution_convert_fusion.1.p_down = bf16[2,704,2048]{2,1,0:T(8,128)(2,1)} fusion(bf16[2,704,512]{2,1,0:T(8,128)(2,1)S(1)} %copy-done.10, bf16[2,512,2048]{2,1,0:T(8,128)(2,1)S(1)} %copy-done.8), kind=kOutput, calls=%fused_computation.2 | convolution fusion | flops 2955673600 | bytes 11403264 | tf_op jit(solution)/shard_map/ehc,ecd->ehd/dot_general | solution.py:613
  144.1 138.3 %shard_map.128 = (bf16[128,2048]{1,0:T(8,128)(2,1)}, bf16[128,2048]{1,0:T(8,128)(2,1)}, f32[8,128]{1,0:T(8,128)}, f32[3,2,704,256]{3,2,1,0:T(8,128)}) custom-call(bf16[2,704,2048]{2,1,0:T(8,128)(2,1)} %convolution_convert_fusion.3.p_gate, bf16[2,704,2048]{2,1,0:T(8,128)(2,1)} %convolution_convert_fusion.2.p_up, ...), custom_call_target="tpu_custom_call" | custom-call | tf_op jit(solution)/shard_map/pallas_call | solution.py:586
  282.5 4.5 %slice_bitcast_fusion = (f32[2,704,256]{2,1,0:T(8,128)}, f32[2,256,704]{1,2,0:T(8,128)}, f32[2,256,704]{1,2,0:T(8,128)}) fusion(f32[3,2,704,256]{3,2,1,0:T(8,128)} %get-tuple-element.51), kind=kLoop, calls=%fused_computation.18 | loop fusion | bytes 8650752 | tf_op jit(solution)/shard_map/squeeze | solution.py:646
  286.9 0.6 slice_bitcast_fusion.3
  287.5 0.8 copy.41
  288.3 0.8 copy.42
  (24 shorter events, 0.1 us)
Async XLA Ops:
  9.1 8.6 %copy-start.4 = (s32[128,6]{0,1:T(8,128)S(1)}, s32[128,6]{0,1:T(8,128)}, u32[]{:S(2)}) copy-start(s32[128,6]{0,1:T(8,128)} %param.16) | copy-start | bytes 9220
  9.1 8.6 %copy-start.5 = (s32[128,6]{0,1:T(8,128)S(1)}, s32[128,6]{0,1:T(8,128)}, u32[]{:S(2)}) copy-start(s32[128,6]{0,1:T(8,128)} %param.15) | copy-start | bytes 9220
  9.1 8.6 %copy-start.6 = (f32[128,6]{0,1:T(8,128)S(1)}, f32[128,6]{0,1:T(8,128)}, u32[]{:S(2)}) copy-start(f32[128,6]{0,1:T(8,128)} %param.14) | copy-start | bytes 9220
  17.8 0.6 copy-start.3
  18.4 93.0 %slice-start = ((s8[5767168]{0:T(1024)(128)(4,1)}), s8[1572864]{0:T(1024)(128)(4,1)S(1)}, s32[]{:S(2)}) async-start(s8[5767168]{0:T(1024)(128)(4,1)} %bitcast.64), calls=%async_computation | async-start | bytes 3145728
  100.2 11.3 %slice-start.1 = ((s8[5767168]{0:T(1024)(128)(4,1)}), s8[4194304]{0:T(1024)(128)(4,1)S(1)}, s32[]{:S(2)}) async-start(s8[5767168]{0:T(1024)(128)(4,1)} %bitcast.64), calls=%async_computation.1 | async-start | bytes 8388608
  122.6 1.0 copy-start.2
  123.5 5.6 %copy-start.9 = (bf16[2,512,2048]{2,1,0:T(8,128)(2,1)S(1)}, bf16[2,512,2048]{2,1,0:T(8,128)(2,1)}, u32[]{:S(2)}) copy-start(bf16[2,512,2048]{2,1,0:T(8,128)(2,1)} %get-tuple-element.43) | copy-start | bytes 12582916
  129.1 5.0 %copy-start.11 = (bf16[2,512,704]{2,1,0:T(8,128)(2,1)S(1)}, bf16[2,512,704]{2,1,0:T(8,128)(2,1)}, u32[]{:S(2)}) copy-start(bf16[2,512,704]{2,1,0:T(8,128)(2,1)} %get-tuple-element.53) | copy-start | bytes 4325380
  134.2 5.1 %copy-start.8 = (bf16[2,512,2048]{2,1,0:T(8,128)(2,1)S(1)}, bf16[2,512,2048]{2,1,0:T(8,128)(2,1)}, u32[]{:S(2)}) copy-start(bf16[2,512,2048]{2,1,0:T(8,128)(2,1)} %get-tuple-element.41) | copy-start | bytes 12582916
  134.2 5.1 %copy-start.10 = (bf16[2,704,512]{2,1,0:T(8,128)(2,1)S(1)}, bf16[2,704,512]{2,1,0:T(8,128)(2,1)}, u32[]{:S(2)}) copy-start(bf16[2,704,512]{2,1,0:T(8,128)(2,1)} %get-tuple-element.44) | copy-start | bytes 4325380
  282.5 4.5 %copy-start.7 = (f32[8,128]{1,0:T(8,128)S(1)}, f32[8,128]{1,0:T(8,128)}, u32[]{:S(2)}) copy-start(f32[8,128]{1,0:T(8,128)} %get-tuple-element.50) | copy-start | bytes 12292
  282.5 5.1 %copy-start.1 = (bf16[128,2048]{1,0:T(8,128)(2,1)S(1)}, bf16[128,2048]{1,0:T(8,128)(2,1)}, u32[]{:S(2)}) copy-start(bf16[128,2048]{1,0:T(8,128)(2,1)} %get-tuple-element.63) | copy-start | bytes 1572868
  282.5 5.9 %copy-start = (bf16[128,2048]{1,0:T(8,128)(2,1)S(1)}, bf16[128,2048]{1,0:T(8,128)(2,1)}, u32[]{:S(2)}) copy-start(bf16[128,2048]{1,0:T(8,128)(2,1)} %get-tuple-element.64) | copy-start | bytes 1572868
where the time goes:
time: 290 us; the launch traced here: 289 us
  Pallas kernels  220 us (76%)
  matrix products  43 us (15%)
  local copies, waits for them, and re-layouts  25.4 us (9%)
    pallas_call x1, Pallas kernels, reduce_all(): pl.pallas_call(reduce_kernel, out_shape=(jax.ShapeDtypeStruct((128, d), B...  138 us
    pallas_call x1, Pallas kernels, forward(): pl.pallas_call(forward_kernel, out_shape=(jax.ShapeDtypeStruct((2, 512, d...  81.7 us
    dot_general x7, matrix products, dot(): return jnp.einsum(spec, a, b, preferred_element_type=F32)  43 us
    unnamed x32, local copies, waits for them, and re-layouts  19.6 us

commit v1 on v0

v1 whole, which is shorter than its diff:
```python
import functools

import jax
import jax.numpy as jnp
from jax import lax
from jax.experimental import pallas as pl
from jax.experimental.pallas import tpu as pltpu
from jax.sharding import PartitionSpec as P

MESH = pl.DeviceIdType.MESH
F32 = jnp.float32
BF16 = jnp.bfloat16
NX = 4
NY = 4
H_ROWS = 704
W_COLS = 256


def slot_of(dx, dz, dc):
    return (dx % NX) * 4 + (dz % 2) * 2 + (dc % 2)


class Place:
    def __init__(self):
        e = lax.axis_index("expert")
        q = lax.axis_index("dp")
        self.e, self.q = e, q
        self.x, self.zl, self.c = e // 4, (e // 2) % 2, e % 2
        self.y, self.zh = q // 2, q % 2

    def group(self, dx=0, dz=0, dc=0):
        x = lax.rem(self.x + (dx % NX), NX) if dx % NX else self.x
        z = 1 - self.zl if dz % 2 else self.zl
        c = 1 - self.c if dc % 2 else self.c
        return (x * 4 + z * 2 + c, self.q)

    def col(self, dy=0, dz=0):
        y = lax.rem(self.y + (dy % NY), NY) if dy % NY else self.y
        z = 1 - self.zh if dz % 2 else self.zh
        return (self.e, y * 2 + z)


def enter(peers):
    barrier = pltpu.get_barrier_semaphore()
    for peer in peers:
        pl.semaphore_signal(barrier, inc=1, device_id=peer, device_id_type=MESH)
    pl.semaphore_wait(barrier, len(peers))


class Sent:
    def __init__(self, owner, i, dst):
        self.owner, self.i, self.dst = owner, i, dst

    def again(self):
        dst = self.dst()
        return pltpu.make_async_remote_copy(
            src_ref=dst,
            dst_ref=dst,
            send_sem=self.owner.send_sem.at[self.i],
            recv_sem=self.owner.recv_sem.at[self.i],
            device_id=self.owner.home,
            device_id_type=MESH,
        )

    def wait_recv(self):
        self.again().wait_recv()

    def wait_send(self):
        self.again().wait_send()


class Sends:
    def __init__(self, send_sem, recv_sem, place):
        self.send_sem, self.recv_sem = send_sem, recv_sem
        self.home = (place.e, place.q)
        self.made = []

    def start(self, src, dst, peer):
        i = len(self.made)
        pltpu.make_async_remote_copy(
            src_ref=src,
            dst_ref=dst(),
            send_sem=self.send_sem.at[i],
            recv_sem=self.recv_sem.at[i],
            device_id=peer,
            device_id_type=MESH,
        ).start()
        copy = Sent(self, i, dst)
        self.made.append(copy)
        return copy

    def drain(self):
        for copy in self.made:
            copy.wait_send()


def dot_nn(a, b):
    return jnp.dot(a, b, preferred_element_type=F32)


def dot_nt(a, b):
    return lax.dot_general(a, b, (((1,), (1,)), ((), ())), preferred_element_type=F32)


def dot_tn(a, b):
    return lax.dot_general(a, b, (((0,), (0,)), ((), ())), preferred_element_type=F32)


GROUP = [(dx, dz, dc) for dx in range(NX) for dz in range(2) for dc in range(2)]
A = (0, 64)
B = (64, 128)
A0, A1, B0, B1 = (0, 32), (32, 64), (64, 96), (96, 128)


def gather_rows(sends, place, own, buf):
    arrived = {}

    def push(dx, dz, dc, rows, ddx=0, ddz=0, ddc=0):
        lo, hi = rows
        here = own if (dx, dz, dc) == (0, 0, 0) else buf.at[slot_of(dx, dz, dc)]
        there = ((dx - ddx) % NX, (dz - ddz) % 2, (dc - ddc) % 2)
        arrived[there + (rows,)] = sends.start(
            here.at[pl.ds(lo, hi - lo)],
            lambda: buf.at[slot_of(*there), pl.ds(lo, hi - lo)],
            place.group(ddx, ddz, ddc),
        )

    def take(dx, dz, rows):
        arrived[(dx % NX, dz % 2, 0, rows)].wait_recv()
        push(dx % NX, dz % 2, 0, rows, ddc=1)

    yield
    push(0, 0, 0, B, ddz=1)
    push(0, 0, 0, A, ddx=1)
    push(0, 0, 0, A, ddx=-1)
    push(0, 0, 0, B, ddx=1)
    push(0, 0, 0, B, ddx=-1)
    push(0, 0, 0, A, ddz=1)
    push(0, 0, 0, (0, 128), ddc=1)
    yield
    take(0, 1, B)
    push(0, 1, 0, B, ddx=1)
    push(0, 1, 0, B, ddx=-1)
    yield
    take(1, 0, A)
    push(1, 0, 0, A0, ddx=-1)
    push(1, 0, 0, A, ddz=1)
    take(-1, 0, A)
    push(3, 0, 0, A1, ddx=1)
    push(3, 0, 0, A, ddz=1)
    yield
    take(1, 0, B)
    push(1, 0, 0, B0, ddx=-1)
    take(-1, 0, B)
    push(3, 0, 0, B1, ddx=1)
    take(0, 1, A)
    yield
    take(1, 1, B)
    push(1, 1, 0, B0, ddx=-1)
    take(-1, 1, B)
    push(3, 1, 0, B1, ddx=1)
    take(2, 0, A0)
    push(2, 0, 0, A0, ddz=1)
    take(2, 0, A1)
    push(2, 0, 0, A1, ddz=1)
    yield
    take(1, 1, A)
    take(3, 1, A)
    take(2, 0, B0)
    take(2, 0, B1)
    take(2, 1, B0)
    take(2, 1, B1)
    take(2, 1, A0)
    take(2, 1, A1)
    yield
    for key in list(arrived):
        if key[2] == 1:
            arrived[key].wait_recv()
    yield


def forward_kernel(
    tok, cot, meta, wg_hbm, wu_hbm, wd_hbm,
    routed_o, dy_o, pre_o, hidden_o, rows_o, gates_o, pick,
    tok_all, cot_all, meta_all, wg, wu, wd, routed, y_rows, dy, pre, hidden, hidden_t, gate_col,
    send_sem, recv_sem, copy_sem,
):
    place = Place()
    enter([place.group(*r) for r in GROUP[1:]])
    copies = []

    def local(src, dst):
        copy = pltpu.make_async_copy(src, dst, copy_sem.at[len(copies)])
        copy.start()
        copies.append(copy)
        return copy

    tok_sends = Sends(send_sem.at[pl.ds(0, 48)], recv_sem.at[pl.ds(0, 48)], place)
    cot_sends = Sends(send_sem.at[pl.ds(48, 48)], recv_sem.at[pl.ds(48, 48)], place)
    sends = Sends(send_sem.at[pl.ds(96, 16)], recv_sem.at[pl.ds(96, 16)], place)
    metas = []
    for r in GROUP[1:]:
        to = slot_of(-r[0], r[1], r[2])
        metas.append(sends.start(meta, lambda to=to: meta_all.at[to], place.group(*r)))
    first = gather_rows(tok_sends, place, tok, tok_all)
    second = gather_rows(cot_sends, place, cot, cot_all)
    next(first)
    next(second)
    next(first)
    own = [local(tok, tok_all.at[0]), local(cot, cot_all.at[0]), local(meta, meta_all.at[0])]
    weights = [local(wg_hbm, wg), local(wu_hbm, wu), local(wd_hbm, wd)]
    next(first)
    for copy in metas:
        copy.wait_recv()
    for copy in own:
        copy.wait()
    slot = (lax.broadcasted_iota(jnp.int32, (64, 128), 0) + place.e * 64).astype(F32)

    @pl.loop(0, 16)
    def _(j):
        total = jnp.zeros((64, 128), F32)
        gate = jnp.zeros((64, 128), F32)
        for k in range(6):
            hit = slot == jnp.broadcast_to(meta_all[j, k : k + 1], (64, 128))
            total = total + jnp.where(hit, 1.0, 0.0)
            row = jnp.broadcast_to(meta_all[j, 8 + k : 9 + k], (64, 128))
            gate = gate + jnp.where(hit, row, 0.0)
        pick[j] = total.astype(BF16)
        gate_col[j] = jnp.broadcast_to(jnp.sum(gate, axis=1, keepdims=True), (64, 128))

    next(first)
    next(first)
    next(first)
    next(second)
    for _ in first:
        pass
    next(second)

    def rows32(j):
        return pl.ds(pl.multiple_of(j * 32, 32), 32)

    @pl.loop(0, 16)
    def _(j):
        got = jnp.dot(pick[j], tok_all[j], preferred_element_type=F32).astype(BF16)
        routed[0, rows32(j)] = got[0:32]
        routed[1, rows32(j)] = got[32:64]

    routed_out = local(routed, routed_o)
    next(second)
    for copy in weights:
        copy.wait()

    def up(e):
        pre[e, 0] = dot_nt(routed[e], wg[e])
        pre[e, 1] = dot_nt(routed[e], wu[e])

        @pl.loop(0, 16)
        def _(i):
            at = rows32(i)
            gate = pre[e, 0, at]
            hidden[e, at] = (gate * jax.nn.sigmoid(gate) * pre[e, 1, at]).astype(BF16)

        local(pre.at[e], pre_o.at[e])

    def down(e):
        hidden_t[e] = hidden[e].T
        local(hidden_t.at[e], hidden_o.at[e])
        for n in range(2):
            at = pl.ds(n * 1024, 1024)
            y_rows[e, :, at] = jnp.dot(
                hidden[e], wd[e, :, at], preferred_element_type=F32
            ).astype(BF16)

    up(0)
    next(second)
    up(1)
    next(second)
    down(0)
    next(second)
    down(1)
    tok_sends.drain()

    def both(ref, j):
        return jnp.concatenate([ref[0, rows32(j)], ref[1, rows32(j)]], axis=0)

    @pl.loop(0, 16)
    def _(j):
        scaled = (both(y_rows, j).astype(F32) * gate_col[j, :, 0:1]).astype(BF16)
        tok_all[j] = lax.dot_general(
            pick[j], scaled, (((0,), (0,)), ((), ())), preferred_element_type=F32
        ).astype(BF16)

    local(tok_all, rows_o)
    for _ in second:
        pass

    @pl.loop(0, 16)
    def _(j):
        got = jnp.dot(pick[j], cot_all[j], preferred_element_type=F32)
        by_slot = jnp.sum(got * both(y_rows, j).astype(F32), axis=1, keepdims=True)
        scaled = (got * gate_col[j, :, 0:1]).astype(BF16)
        dy[0, rows32(j)] = scaled[0:32]
        dy[1, rows32(j)] = scaled[32:64]
        by_slot = jnp.broadcast_to(by_slot, (64, 128))
        parts = []
        for k in range(6):
            hit = slot == jnp.broadcast_to(meta_all[j, k : k + 1], (64, 128))
            parts.append(jnp.sum(jnp.where(hit, by_slot, 0.0), axis=0, keepdims=True))
        parts.append(jnp.zeros((2, 128), F32))
        gates_o[j] = jnp.concatenate(parts, axis=0)

    local(dy, dy_o)
    for copy in copies[6:]:
        copy.wait()
    cot_sends.drain()
    sends.drain()


def forward(tok, cot, meta, w_gate, w_up, w_down):
    d = tok.shape[1]
    hbm = pl.BlockSpec(memory_space=pl.ANY)
    vmem = pl.BlockSpec(memory_space=pltpu.VMEM)
    return pl.pallas_call(
        forward_kernel,
        out_shape=(
            jax.ShapeDtypeStruct((2, 512, d), BF16),
            jax.ShapeDtypeStruct((2, 512, d), BF16),
            jax.ShapeDtypeStruct((2, 2, 512, H_ROWS), F32),
            jax.ShapeDtypeStruct((2, H_ROWS, 512), BF16),
            jax.ShapeDtypeStruct((16, 128, d), BF16),
            jax.ShapeDtypeStruct((16, 8, 128), F32),
            jax.ShapeDtypeStruct((16, 64, 128), BF16),
        ),
        in_specs=[hbm] * 6,
        out_specs=(hbm, hbm, hbm, hbm, hbm, vmem, vmem),
        scratch_shapes=[
            pltpu.VMEM((16, 128, d), BF16),
            pltpu.VMEM((16, 128, d), BF16),
            pltpu.VMEM((16,) + meta.shape, F32),
            pltpu.VMEM(w_gate.shape, BF16),
            pltpu.VMEM(w_up.shape, BF16),
            pltpu.VMEM(w_down.shape, BF16),
            pltpu.VMEM((2, 512, d), BF16),
            pltpu.VMEM((2, 512, d), BF16),
            pltpu.VMEM((2, 512, d), BF16),
            pltpu.VMEM((2, 2, 512, H_ROWS), F32),
            pltpu.VMEM((2, 512, H_ROWS), BF16),
            pltpu.VMEM((2, H_ROWS, 512), BF16),
            pltpu.VMEM((16, 64, 128), F32),
            pltpu.SemaphoreType.DMA((112,)),
            pltpu.SemaphoreType.DMA((112,)),
            pltpu.SemaphoreType.DMA((16,)),
        ],
        compiler_params=pltpu.CompilerParams(
            collective_id=0, has_side_effects=True, vmem_limit_bytes=62 * 2**20
        ),
    )(tok, cot, meta, w_gate, w_up, w_down)


def add_into(dst, terms, chunk):
    rows = dst.shape[0]

    @pl.loop(0, rows // chunk)
    def _(i):
        at = pl.ds(pl.multiple_of(i * chunk, chunk), chunk)
        total = terms[0][at].astype(F32)
        for term in terms[1:]:
            total = total + term[at].astype(F32)
        dst[at] = total.astype(dst.dtype)


class Tree:
    def __init__(self, sends, peer, part, land, out, chunk):
        self.sends, self.peer, self.part = sends, peer, part
        self.land, self.out, self.chunk = land, out, chunk

    def open(self):
        s, p, peer = self.sends, self.part, self.peer
        self.far = [
            s.start(p(2, 0), lambda: self.land(0, 0), peer(-1)),
            s.start(p(2, 1), lambda: self.land(0, 1), peer(1)),
        ]
        self.near = [
            s.start(p(1, 0), lambda: self.land(1, 0), peer(1)),
            s.start(p(-1, 1), lambda: self.land(1, 1), peer(-1)),
        ]

    def relay(self):
        self.via = []
        for h, d in ((0, -1), (1, 1)):
            self.far[h].wait_recv()
            add_into(self.out(h), [self.part(d, h), self.land(0, h)], self.chunk)
            self.via.append(self.sends.start(self.out(h), lambda h=h: self.land(2, h), self.peer(d)))

    def close(self, h):
        self.near[h].wait_recv()
        self.via[h].wait_recv()
        return [self.part(0, h), self.land(1, h), self.land(2, h)]


Y_FIRST = ((2, 0), (0, 0), (0, 1), (1, 1))
Z_FIRST = ((2, 1), (1, 0))


def backward_kernel(
    routed_hbm, dy_hbm, pre_hbm, hidden_hbm, wg_hbm, wu_hbm, wd_hbm, o_first, gates_in, pick,
    out_first, out_second, gates_out, grads_out, p_hbm, o_own, land_s,
    land_y, land_z, land_d, land_dz, land_xb, land_zb, gates_land,
    send_sem, recv_sem, load_sem,
):
    place = Place()
    loads = []

    def load(src, dst):
        copy = pltpu.make_async_copy(src, dst, load_sem.at[len(loads)])
        copy.start()
        loads.append(copy)
        return copy

    rows_out = (out_first, out_second)
    sends = Sends(send_sem, recv_sem, place)

    def yy(d):
        return lax.rem(place.y + (d % NY), NY) if d % NY else place.y

    def p_slice(m, e, d, z):
        at = pl.multiple_of((yy(d) * 2 + z) * W_COLS, W_COLS)
        return p_hbm.at[m, e, :, pl.ds(at, W_COLS)]

    trees = {}
    down_z = {}

    def open_partial(m, e):
        if (m, e) in Y_FIRST:
            i = Y_FIRST.index((m, e))
            tree = Tree(
                sends, place.col,
                lambda d, h: p_slice(m, e, d, h),
                lambda k, h: land_y.at[i, k, h],
                None, 64,
            )
            tree.open()
            trees[i] = tree
        else:
            i = Z_FIRST.index((m, e))
            for d in (2, 1, 3, 0):
                down_z[i, d] = sends.start(
                    p_slice(m, e, d, 1 - place.zh), lambda d=d: land_dz.at[i, d], place.col(0, 1)
                )

    shares = {}

    def first_phase(
        routed, dy, pre, hidden_t, wg, wu, wd, dhd, dg, du, dg_t, du_t, stage, o_stage
    ):
        ld = [
            load(hidden_hbm, hidden_t), load(dy_hbm, dy), load(wd_hbm.at[0], wd),
            load(pre_hbm.at[0], pre), load(routed_hbm, routed),
            load(wg_hbm.at[0], wg), load(wu_hbm.at[0], wu),
        ]
        peers = [place.group(*r) for r in GROUP[1:]]
        enter(peers + [place.col(1), place.col(-1), place.col(0, 1)])
        for dx in range(NX):
            for dz in range(2):
                i = dx * 2 + dz
                shares[0, i] = sends.start(
                    o_first.at[slot_of(dx, dz, 1)], lambda i=i: land_s.at[0, i],
                    place.group(0, 0, 1),
                )
        gate_sends = []
        for r in GROUP[1:]:
            to = slot_of(-r[0], r[1], r[2])
            gate_sends.append(
                sends.start(
                    gates_in.at[slot_of(*r)], lambda to=to: gates_land.at[to], place.group(*r)
                )
            )
        pending = []

        def flush():
            for copies, m, e in pending:
                for copy in copies:
                    copy.wait()
                open_partial(m, e)
            pending.clear()

        def partial(m, e, left, right):
            copies = []
            before = list(pending)
            for n in range(2):
                for entry in before:
                    entry[0][n].wait()

                @pl.loop(0, 2)
                def _(k):
                    at = pl.ds(pl.multiple_of(k * 512, 512), 512)
                    src = pl.ds(pl.multiple_of(n * 1024 + k * 512, 512), 512)
                    stage[n, :, at] = dot_nn(left[...], right[:, src]).astype(BF16)

                copies.append(
                    load(stage.at[n], p_hbm.at[m, e, :, pl.ds(n * 1024, 1024)])
                )
            for entry in before:
                open_partial(entry[1], entry[2])
                pending.remove(entry)
            pending.append((copies, m, e))

        ld[0].wait()
        ld[1].wait()
        partial(2, 0, hidden_t.at[0], dy.at[0])
        partial(2, 1, hidden_t.at[1], dy.at[1])
        for e in range(2):
            if e == 0:
                ld[2].wait()
                ld[3].wait()
                ld[4].wait()
                ld[5].wait()
                ld[6].wait()
            else:
                next_wd.wait()
                next_pre.wait()
            dhd[...] = dot_nt(dy[e], wd[...])
            if e == 0:
                next_wd = load(wd_hbm.at[1], wd)

            @pl.loop(0, 16)
            def _(i):
                at = pl.ds(pl.multiple_of(i * 32, 32), 32)
                gate = pre[0, at]
                s = jax.nn.sigmoid(gate)
                back = dhd[at]
                dg[at] = (back * pre[1, at] * s * (1.0 + gate * (1.0 - s))).astype(BF16)
                du[at] = (back * gate * s).astype(BF16)

            if e == 0:
                next_pre = load(pre_hbm.at[1], pre)
            dg_t[...] = dg[...].T
            du_t[...] = du[...].T
            partial(0, e, dg_t, routed.at[e])
            partial(1, e, du_t, routed.at[e])
            if e == 1:
                for copy in next_w:
                    copy.wait()

            @pl.loop(0, 4)
            def _(n):
                at = pl.ds(pl.multiple_of(n * 512, 512), 512)
                total = dot_nn(dg[...], wg[:, at]) + dot_nn(du[...], wu[:, at])
                routed[e, :, at] = total.astype(BF16)

            if e == 0:
                next_w = [load(wg_hbm.at[1], wg), load(wu_hbm.at[1], wu)]
        for entry in pending:
            for copy in entry[0]:
                copy.wait()
            open_partial(entry[1], entry[2])

        def back_rows(j):
            at = pl.ds(pl.multiple_of(j * 32, 32), 32)
            rows = jnp.concatenate([routed[0, at], routed[1, at]], axis=0)
            return dot_tn(pick[j], rows).astype(BF16)

        @pl.loop(0, 8)
        def _(i):
            at = pl.ds(pl.multiple_of(lax.rem(i, 4) * 128, 128), 128)
            dy[i // 4, at] = back_rows(i * 2 + 1)

        for i in range(8):
            shares[1, i] = sends.start(
                dy.at[i // 4, pl.ds((i % 4) * 128, 128)], lambda i=i: land_s.at[1, i],
                place.group(0, 0, 1),
            )
        outs = []
        for i in range(8):
            if i >= 2:
                outs[i - 2].wait()
            o_stage[i % 2] = back_rows(i * 2)
            outs.append(load(o_stage.at[i % 2], o_own.at[i]))
        for copy in outs[6:]:
            copy.wait()
        for i in range(8):
            shares[1, i].wait_send()
        for copy in gate_sends:
            copy.wait_recv()
        total = gates_in[0]
        for i in range(1, 16):
            total = total + gates_land[i]
        gates_out[...] = total

    def second_phase(own_p, out_y, out_z, t_down, out_d, t_rows, s_stage, out_xb, v_rows):
        own_rows = []
        for r in range(2):
            for i in range(8):
                src = o_first.at[i * 2] if r == 0 else o_own.at[i]
                own_rows.append(load(src, t_rows.at[r, i]))
        own_loads = {}
        for i, (m, e) in enumerate(Y_FIRST):
            own_loads[i] = [
                load(p_slice(m, e, -1, 0), own_p.at[i, 0]),
                load(p_slice(m, e, 1, 1), own_p.at[i, 1]),
                load(p_slice(m, e, 0, 0), own_p.at[i, 2]),
                load(p_slice(m, e, 0, 1), own_p.at[i, 3]),
            ]
        down_loads = {}
        for i, (m, e) in enumerate(Z_FIRST):
            down_loads[i] = [load(p_slice(m, e, d, place.zh), t_down.at[i, d]) for d in range(NY)]

        row_state = {}

        def rows_start(r):
            gets = []
            for i in range(8):
                shares[r, i].wait_recv()
            for i in range(9):
                if i < 8:
                    gets.append(load(land_s.at[r, i], s_stage.at[i % 2]))
                if i > 0:
                    gets[i - 1].wait()
                    own_rows[r * 8 + i - 1].wait()
                    dst = t_rows.at[r, i - 1]
                    add_into(dst, [dst, s_stage.at[(i - 1) % 2]], 32)
            made = []
            for dz in (1, 0):
                tree = Tree(
                    sends, place.group,
                    lambda d, h, dz=dz: t_rows.at[r, (d % NX) * 2 + dz, pl.ds(64 * h, 64)],
                    lambda k, h, dz=dz: land_xb.at[r, dz, k, h],
                    lambda h, dz=dz: out_xb.at[r, dz, h],
                    32,
                )
                tree.open()
                made.append(tree)
            row_state[r] = made

        def rows_mid(r):
            for tree in row_state[r]:
                tree.relay()

        def rows_end(r):
            for h in range(2):
                add_into(v_rows.at[r, 1, pl.ds(64 * h, 64)], row_state[r][0].close(h), 32)
            copy = sends.start(v_rows.at[r, 1], lambda: land_zb.at[r], place.group(0, 1, 0))
            for h in range(2):
                add_into(v_rows.at[r, 0, pl.ds(64 * h, 64)], row_state[r][1].close(h), 32)
            return copy

        def rows_last(r, copy):
            copy.wait_recv()
            add_into(rows_out[r], [v_rows.at[r, 0], land_zb.at[r]], 32)

        def down_mid(i):
            for copy in down_loads[i]:
                copy.wait()
            for d in (2, 1, 3, 0):
                down_z[i, d].wait_recv()
                add_into(t_down.at[i, d], [t_down.at[i, d], land_dz.at[i, d]], 64)
            half = H_ROWS // 2
            tree = Tree(
                sends, place.col,
                lambda d, h: t_down.at[i, d % NY, pl.ds(half * h, half)],
                lambda k, h: land_d.at[i, k, pl.ds(half * h, half)],
                lambda h: out_d.at[i, pl.ds(half * h, half)],
                32,
            )
            tree.open()
            return tree

        def down_end(i, tree):
            m, e = Z_FIRST[i]
            half = H_ROWS // 2
            for h in range(2):
                add_into(grads_out.at[m, e, pl.ds(half * h, half)], tree.close(h), 32)

        def y_relay(i):
            for copy in own_loads[i]:
                copy.wait()
            trees[i].part = lambda d, h: own_p.at[i, {-1: 0, 1: 1, 0: 2 + h}[d]]
            trees[i].out = lambda h: out_y.at[i, h]
            trees[i].relay()

        def y_end(i):
            m, e = Y_FIRST[i]
            for h in range(2):
                terms = trees[i].close(h)

                @pl.when(place.zh != h)
                def _():
                    add_into(out_z.at[i], terms, 64)

                @pl.when(place.zh == h)
                def _():
                    add_into(grads_out.at[m, e], terms, 64)

            return sends.start(out_z.at[i], lambda: land_z.at[i], place.col(0, 1))

        def z_end(i, copy):
            m, e = Y_FIRST[i]
            copy.wait_recv()
            dst = grads_out.at[m, e]
            add_into(dst, [dst, land_z.at[i]], 64)

        rows_start(0)
        y_relay(0)
        rows_start(1)
        d0 = down_mid(0)
        rows_mid(0)
        y_relay(1)
        rows_mid(1)
        y_relay(2)
        r0 = rows_end(0)
        d1 = down_mid(1)
        y_relay(3)
        z0 = y_end(0)
        r1 = rows_end(1)
        d0.relay()
        z1 = y_end(1)
        rows_last(0, r0)
        d1.relay()
        z2 = y_end(2)
        rows_last(1, r1)
        z_end(0, z0)
        down_end(0, d0)
        z3 = y_end(3)
        z_end(1, z1)
        down_end(1, d1)
        z_end(2, z2)
        z_end(3, z3)
        for copy in sends.made:
            if all(copy is not c for (r, _), c in shares.items() if r == 1):
                copy.wait_send()

    def buf(*shape):
        return pltpu.VMEM(shape, BF16)

    d = o_first.shape[-1]
    slab = (H_ROWS, W_COLS)
    pl.run_scoped(
        first_phase,
        buf(2, 512, d), buf(2, 512, d), pltpu.VMEM((2, 512, H_ROWS), F32), buf(2, H_ROWS, 512),
        buf(H_ROWS, d), buf(H_ROWS, d), buf(H_ROWS, d), pltpu.VMEM((512, H_ROWS), F32),
        buf(512, H_ROWS), buf(512, H_ROWS), buf(H_ROWS, 512), buf(H_ROWS, 512),
        buf(2, H_ROWS, 1024), buf(2, 128, d),
    )
    pl.run_scoped(
        second_phase,
        buf(4, 4, *slab), buf(4, 2, *slab), buf(4, *slab), buf(2, 4, *slab), buf(2, *slab),
        buf(2, 8, 128, d), buf(2, 128, d), buf(2, 2, 2, 64, d), buf(2, 2, 128, d),
    )


def backward(*operands):
    d = operands[0].shape[-1]
    n = 192
    hbm = pl.BlockSpec(memory_space=pl.ANY)
    vmem = pl.BlockSpec(memory_space=pltpu.VMEM)
    slab = (H_ROWS, W_COLS)

    def buf(*shape):
        return pltpu.VMEM(shape, BF16)

    return pl.pallas_call(
        backward_kernel,
        out_shape=(
            jax.ShapeDtypeStruct((128, d), BF16),
            jax.ShapeDtypeStruct((128, d), BF16),
            jax.ShapeDtypeStruct((8, 128), F32),
            jax.ShapeDtypeStruct((3, 2) + slab, F32),
            jax.ShapeDtypeStruct((3, 2, H_ROWS, d), BF16),
            jax.ShapeDtypeStruct((8, 128, d), BF16),
            jax.ShapeDtypeStruct((2, 8, 128, d), BF16),
        ),
        in_specs=[hbm] * 8 + [vmem] * 2,
        out_specs=(vmem,) * 4 + (hbm,) * 3,
        scratch_shapes=[
            buf(4, 3, 2, *slab), buf(4, *slab), buf(2, 3, *slab), buf(2, 4, *slab),
            buf(2, 2, 3, 2, 64, d), buf(2, 128, d),
            pltpu.VMEM((16, 8, 128), F32),
            pltpu.SemaphoreType.DMA((n,)),
            pltpu.SemaphoreType.DMA((n,)),
            pltpu.SemaphoreType.DMA((112,)),
        ],
        compiler_params=pltpu.CompilerParams(
            collective_id=1, has_side_effects=True, vmem_limit_bytes=63 * 2**20
        ),
    )(*operands)[:4]


def shards(tokens, cotangent, route_gates, expert_ids, slot_index, w_gate, w_up, w_down):
    target = (expert_ids * 32 + slot_index).astype(F32).T
    meta = jnp.zeros((16, 128), F32).at[0:6].set(target).at[8:14].set(route_gates.T)
    wg, wu = w_gate.transpose(0, 2, 1), w_up.transpose(0, 2, 1)
    routed, grad_rows, pre, hidden_t, o_out, gates_in, pick = forward(
        tokens, cotangent, meta, wg, wu, w_down
    )
    out, grad, gates, grads = backward(
        routed, grad_rows, pre, hidden_t, wg, wu, w_down, o_out, gates_in, pick
    )
    return (
        out,
        grad,
        gates[0:6].T,
        grads[0].transpose(0, 2, 1),
        grads[1].transpose(0, 2, 1),
        grads[2],
    )


def solution(mesh):
    row = P(("expert", "dp"), None)
    weight = P("expert", None, None)
    return jax.shard_map(
        shards,
        mesh=mesh,
        in_specs=(row, row, row, row, row, weight, weight, weight),
        out_specs=(row, row, row, P("expert", "dp", None), P("expert", "dp", None), P("expert", None, "dp")),
        check_vma=False,
    )
```

time: 290 us -> 260 us (0.90); the launches traced: 289 us -> 256 us
  matrix products: 43 us -> 0 us
  Pallas kernels: 220 us -> 246 us
  local copies, waits for them, and re-layouts: 25.4 us -> 8.7 us
    dot_general x7 -> x0, matrix products: 43 us -> none  [dot(): return jnp.einsum(spec, a, b, preferred_element_type=F32)]
    pallas_call x1, Pallas kernels: 138 us -> 164 us  [backward(): pl.pallas_call(backward_kernel, out_shape=(jax.ShapeDtypeStruct((128, d),...]
    unnamed x32 -> x8, local copies, waits for them, and re-layouts: 19.6 us -> 2.19 us
where the time goes in v1:
time: 260 us; the launch traced here: 256 us
  Pallas kernels  246 us (95%)
  local copies, waits for them, and re-layouts  8.7 us (3%)
    pallas_call x1, Pallas kernels, backward(): pl.pallas_call(backward_kernel, out_shape=(jax.ShapeDtypeStruct((128, d),...  164 us
    pallas_call x1, Pallas kernels, forward(): pl.pallas_call(forward_kernel, out_shape=(jax.ShapeDtypeStruct((2, 512, d...  81.5 us

profile of v1, /device:TPU:1, one launch (start us, length us, event | category | flops | bytes accessed | tf_op | source)
XLA Modules:
  0.0 255.9 jit_solution(5829783235786276476)
XLA Ops:
  0.6 0.7 convert_bitcast_fusion
  1.3 0.8 scatter.9.meta
  2.1 0.0 copy-start.2
  2.1 0.6 copy-done.2
  2.7 81.5 %shard_map.127 = (bf16[2,512,2048]{2,1,0:T(8,128)(2,1)}, bf16[2,512,2048]{2,1,0:T(8,128)(2,1)}, f32[2,2,512,704]{3,2,1,0:T(8,128)}, bf16[2,704,512]{2,1,0:T(8,12...) custom-call(bf16[128,2048]{1,0:T(8,128)(2,1)} %tok.1, ...), custom_call_target="tpu_custom_call" | custom-call | tf_op jit(solution)/shard_map/pallas_call | solution.py:323
  84.2 164.4 %shard_map.128 = (bf16[128,2048]{1,0:T(8,128)(2,1)}, bf16[128,2048]{1,0:T(8,128)(2,1)}, f32[8,128]{1,0:T(8,128)}, f32[3,2,704,256]{3,2,1,0:T(8,128)}, bf16[3,2,7...) custom-call(bf16[2,512,2048]{2,1,0:T(8,128)(2,1)} %get-tuple-element.41.routed_hbm, ...), custom_call_target="tpu_custom_call" | custom-call | tf_op jit(solution)/shard_map/pallas_call | solution.py:761
  248.6 1.3 slice_bitcast_fusion.3
  249.8 0.0 copy-start.1
  249.8 0.0 copy-start
  249.8 4.5 %slice_bitcast_fusion = (f32[2,704,256]{2,1,0:T(8,128)}, f32[2,256,704]{1,2,0:T(8,128)}, f32[2,256,704]{1,2,0:T(8,128)}) fusion(f32[3,2,704,256]{3,2,1,0:T(8,128)} %get-tuple-element.51), kind=kLoop, calls=%fused_computation | loop fusion | bytes 8650752 | tf_op jit(solution)/shard_map/squeeze | solution.py:804
  254.3 0.0 copy-done.1
  254.3 0.8 copy.17
  255.1 0.0 copy-done
  255.1 0.8 copy.18
  (1 shorter events, 0.0 us)
Async XLA Ops:
  2.1 0.6 copy-start.2
  249.8 4.5 %copy-start.1 = (bf16[128,2048]{1,0:T(8,128)(2,1)S(1)}, bf16[128,2048]{1,0:T(8,128)(2,1)}, u32[]{:S(2)}) copy-start(bf16[128,2048]{1,0:T(8,128)(2,1)} %get-tuple-element.61) | copy-start | bytes 1572868
  249.8 5.3 %copy-start = (bf16[128,2048]{1,0:T(8,128)(2,1)S(1)}, bf16[128,2048]{1,0:T(8,128)(2,1)}, u32[]{:S(2)}) copy-start(bf16[128,2048]{1,0:T(8,128)(2,1)} %get-tuple-element.62) | copy-start | bytes 1572868

commit v2 on v1

--- a/solution.py
+++ b/solution.py
@@ -173,16 +173,18 @@
     take(2, 1, A0)
     take(2, 1, A1)
     yield
-    for key in list(arrived):
-        if key[2] == 1:
-            arrived[key].wait_recv()
-    yield
+    near = ((0, 0), (0, 1), (1, 0), (3, 0))
+    for first in (True, False):
+        for key in list(arrived):
+            if key[2] == 1 and (key[0:2] in near) == first:
+                arrived[key].wait_recv()
+        yield
 
 
 def forward_kernel(
     tok, cot, meta, wg_hbm, wu_hbm, wd_hbm,
-    routed_o, dy_o, pre_o, hidden_o, rows_o, gates_o, pick,
-    tok_all, cot_all, meta_all, wg, wu, wd, routed, y_rows, dy, pre, hidden, hidden_t, gate_col,
+    routed_o, dy_o, pre_o, hidden_o, totals_o, gates_o, pick,
+    tok_all, cot_all, meta_all, wg, wu, wd, routed, y_rows, dy, pre, hidden, hidden_t, gate_col, land_s,
     send_sem, recv_sem, copy_sem,
 ):
     place = Place()
@@ -197,7 +199,7 @@
 
     tok_sends = Sends(send_sem.at[pl.ds(0, 48)], recv_sem.at[pl.ds(0, 48)], place)
     cot_sends = Sends(send_sem.at[pl.ds(48, 48)], recv_sem.at[pl.ds(48, 48)], place)
-    sends = Sends(send_sem.at[pl.ds(96, 16)], recv_sem.at[pl.ds(96, 16)], place)
+    sends = Sends(send_sem.at[pl.ds(96, 32)], recv_sem.at[pl.ds(96, 32)], place)
     metas = []
     for r in GROUP[1:]:
         to = slot_of(-r[0], r[1], r[2])
@@ -271,31 +273,14 @@
                 hidden[e], wd[e, :, at], preferred_element_type=F32
             ).astype(BF16)
 
-    up(0)
-    next(second)
-    up(1)
-    next(second)
-    down(0)
-    next(second)
-    down(1)
-    tok_sends.drain()
-
     def both(ref, j):
         return jnp.concatenate([ref[0, rows32(j)], ref[1, rows32(j)]], axis=0)
 
-    @pl.loop(0, 16)
-    def _(j):
+    def gated(j):
         scaled = (both(y_rows, j).astype(F32) * gate_col[j, :, 0:1]).astype(BF16)
-        tok_all[j] = lax.dot_general(
-            pick[j], scaled, (((0,), (0,)), ((), ())), preferred_element_type=F32
-        ).astype(BF16)
-
-    local(tok_all, rows_o)
-    for _ in second:
-        pass
-
-    @pl.loop(0, 16)
-    def _(j):
+        return dot_tn(pick[j], scaled)
+
+    def pick_cot(j):
         got = jnp.dot(pick[j], cot_all[j], preferred_element_type=F32)
         by_slot = jnp.sum(got * both(y_rows, j).astype(F32), axis=1, keepdims=True)
         scaled = (got * gate_col[j, :, 0:1]).astype(BF16)
@@ -309,6 +294,45 @@
         parts.append(jnp.zeros((2, 128), F32))
         gates_o[j] = jnp.concatenate(parts, axis=0)
 
+    up(0)
+    next(second)
+    up(1)
+    next(second)
+    down(0)
+    down(1)
+    tok_sends.drain()
+
+    @pl.loop(0, 8)
+    def _(i):
+        tok_all[i * 2 + 1] = gated(i * 2 + 1).astype(BF16)
+
+    shares = [
+        sends.start(tok_all.at[i * 2 + 1], lambda i=i: land_s.at[i], place.group(0, 0, 1))
+        for i in range(8)
+    ]
+    next(second)
+    next(second)
+
+    @pl.loop(0, 8)
+    def _(i):
+        pick_cot(i + 6 * (i // 6))
+
+    for copy in shares:
+        copy.wait_recv()
+
+    @pl.loop(0, 8)
+    def _(i):
+        tok_all[i * 2] = (gated(i * 2) + land_s[i].astype(F32)).astype(BF16)
+
+    for i in range(8):
+        local(tok_all.at[i * 2], totals_o.at[i])
+    for _ in second:
+        pass
+
+    @pl.loop(0, 8)
+    def _(i):
+        pick_cot(6 + i + 2 * (i // 6))
+
     local(dy, dy_o)
     for copy in copies[6:]:
         copy.wait()
@@ -327,7 +351,7 @@
             jax.ShapeDtypeStruct((2, 512, d), BF16),
             jax.ShapeDtypeStruct((2, 2, 512, H_ROWS), F32),
             jax.ShapeDtypeStruct((2, H_ROWS, 512), BF16),
-            jax.ShapeDtypeStruct((16, 128, d), BF16),
+            jax.ShapeDtypeStruct((8, 128, d), BF16),
             jax.ShapeDtypeStruct((16, 8, 128), F32),
             jax.ShapeDtypeStruct((16, 64, 128), BF16),
         ),
@@ -347,12 +371,13 @@
             pltpu.VMEM((2, 512, H_ROWS), BF16),
             pltpu.VMEM((2, H_ROWS, 512), BF16),
             pltpu.VMEM((16, 64, 128), F32),
-            pltpu.SemaphoreType.DMA((112,)),
-            pltpu.SemaphoreType.DMA((112,)),
-            pltpu.SemaphoreType.DMA((16,)),
+            pltpu.VMEM((8, 128, d), BF16),
+            pltpu.SemaphoreType.DMA((128,)),
+            pltpu.SemaphoreType.DMA((128,)),
+            pltpu.SemaphoreType.DMA((32,)),
         ],
         compiler_params=pltpu.CompilerParams(
-            collective_id=0, has_side_effects=True, vmem_limit_bytes=62 * 2**20
+            collective_id=0, has_side_effects=True, vmem_limit_bytes=63 * 2**20
         ),
     )(tok, cot, meta, w_gate, w_up, w_down)
 
@@ -403,9 +428,9 @@
 
 
 def backward_kernel(
-    routed_hbm, dy_hbm, pre_hbm, hidden_hbm, wg_hbm, wu_hbm, wd_hbm, o_first, gates_in, pick,
+    routed_hbm, dy_hbm, pre_hbm, hidden_hbm, wg_hbm, wu_hbm, wd_hbm, t_first, gates_in, pick,
     out_first, out_second, gates_out, grads_out, p_hbm, o_own, land_s,
-    land_y, land_z, land_d, land_dz, land_xb, land_zb, gates_land,
+    land_y, land_z, land_d, land_dz, land_xb, land_zb, gates_land, early_x, early_y,
     send_sem, recv_sem, load_sem,
 ):
     place = Place()
@@ -449,6 +474,7 @@
                 )
 
     shares = {}
+    row_state = {}
 
     def first_phase(
         routed, dy, pre, hidden_t, wg, wu, wd, dhd, dg, du, dg_t, du_t, stage, o_stage
@@ -460,13 +486,40 @@
         ]
         peers = [place.group(*r) for r in GROUP[1:]]
         enter(peers + [place.col(1), place.col(-1), place.col(0, 1)])
-        for dx in range(NX):
-            for dz in range(2):
-                i = dx * 2 + dz
-                shares[0, i] = sends.start(
-                    o_first.at[slot_of(dx, dz, 1)], lambda i=i: land_s.at[0, i],
-                    place.group(0, 0, 1),
-                )
+        for dz in (1, 0):
+            tree = Tree(
+                sends, place.group,
+                lambda d, h, dz=dz: t_first.at[(d % NX) * 2 + dz, pl.ds(64 * h, 64)],
+                lambda k, h, dz=dz: land_xb.at[0, dz, k, h],
+                None, 32,
+            )
+            tree.open()
+            row_state.setdefault(0, []).append(tree)
+        x_loads = [
+            load(t_first.at[6 + dz, pl.ds(0, 64)], early_x.at[dz, 0]) for dz in range(2)
+        ] + [
+            load(t_first.at[2 + dz, pl.ds(64, 64)], early_x.at[dz, 1]) for dz in range(2)
+        ]
+
+        def early_rows():
+            for copy in x_loads:
+                copy.wait()
+            for tree, dz in zip(row_state[0], (1, 0)):
+                tree.part = lambda d, h, dz=dz: early_x.at[dz, h]
+                tree.out = lambda h, dz=dz: early_x.at[dz, h]
+                tree.relay()
+
+        def early_partial():
+            y_loads = [
+                load(p_slice(*Y_FIRST[0], -1, 0), early_y.at[0]),
+                load(p_slice(*Y_FIRST[0], 1, 1), early_y.at[1]),
+            ]
+            for copy in y_loads:
+                copy.wait()
+            trees[0].part = lambda d, h: early_y.at[h]
+            trees[0].out = lambda h: early_y.at[h]
+            trees[0].relay()
+
         gate_sends = []
         for r in GROUP[1:]:
             to = slot_of(-r[0], r[1], r[2])
@@ -549,11 +602,13 @@
                 routed[e, :, at] = total.astype(BF16)
 
             if e == 0:
+                early_rows()
                 next_w = [load(wg_hbm.at[1], wg), load(wu_hbm.at[1], wu)]
         for entry in pending:
             for copy in entry[0]:
                 copy.wait()
             open_partial(entry[1], entry[2])
+        early_partial()
 
         def back_rows(j):
             at = pl.ds(pl.multiple_of(j * 32, 32), 32)
@@ -566,8 +621,8 @@
             dy[i // 4, at] = back_rows(i * 2 + 1)
 
         for i in range(8):
-            shares[1, i] = sends.start(
-                dy.at[i // 4, pl.ds((i % 4) * 128, 128)], lambda i=i: land_s.at[1, i],
+            shares[i] = sends.start(
+                dy.at[i // 4, pl.ds((i % 4) * 128, 128)], lambda i=i: land_s.at[i],
                 place.group(0, 0, 1),
             )
         outs = []
@@ -579,7 +634,7 @@
         for copy in outs[6:]:
             copy.wait()
         for i in range(8):
-            shares[1, i].wait_send()
+            shares[i].wait_send()
         for copy in gate_sends:
             copy.wait_recv()
         total = gates_in[0]
@@ -587,12 +642,9 @@
             total = total + gates_land[i]
         gates_out[...] = total
 
-    def second_phase(own_p, out_y, out_z, t_down, out_d, t_rows, s_stage, out_xb, v_rows):
-        own_rows = []
-        for r in range(2):
-            for i in range(8):
-                src = o_first.at[i * 2] if r == 0 else o_own.at[i]
-                own_rows.append(load(src, t_rows.at[r, i]))
+    def second_phase(own_p, out_z, t_down, out_d, t_rows, own_x, s_stage, out_xb, v_rows):
+        own_rows = [load(o_own.at[i], t_rows.at[i]) for i in range(8)]
+        x_own = [load(t_first.at[dz], own_x.at[dz]) for dz in range(2)]
         own_loads = {}
         for i, (m, e) in enumerate(Y_FIRST):
             own_loads[i] = [
@@ -605,38 +657,41 @@
         for i, (m, e) in enumerate(Z_FIRST):
             down_loads[i] = [load(p_slice(m, e, d, place.zh), t_down.at[i, d]) for d in range(NY)]
 
-        row_state = {}
-
-        def rows_start(r):
+        def rows_start():
             gets = []
             for i in range(8):
-                shares[r, i].wait_recv()
+                shares[i].wait_recv()
             for i in range(9):
                 if i < 8:
-                    gets.append(load(land_s.at[r, i], s_stage.at[i % 2]))
+                    gets.append(load(land_s.at[i], s_stage.at[i % 2]))
                 if i > 0:
                     gets[i - 1].wait()
-                    own_rows[r * 8 + i - 1].wait()
-                    dst = t_rows.at[r, i - 1]
+                    own_rows[i - 1].wait()
+                    dst = t_rows.at[i - 1]
                     add_into(dst, [dst, s_stage.at[(i - 1) % 2]], 32)
             made = []
             for dz in (1, 0):
                 tree = Tree(
                     sends, place.group,
-                    lambda d, h, dz=dz: t_rows.at[r, (d % NX) * 2 + dz, pl.ds(64 * h, 64)],
-                    lambda k, h, dz=dz: land_xb.at[r, dz, k, h],
-                    lambda h, dz=dz: out_xb.at[r, dz, h],
+                    lambda d, h, dz=dz: t_rows.at[(d % NX) * 2 + dz, pl.ds(64 * h, 64)],
+                    lambda k, h, dz=dz: land_xb.at[1, dz, k, h],
+                    lambda h, dz=dz: out_xb.at[dz, h],
                     32,
                 )
                 tree.open()
                 made.append(tree)
-            row_state[r] = made
-
-        def rows_mid(r):
-            for tree in row_state[r]:
+            row_state[1] = made
+
+        def rows_mid():
+            for tree in row_state[1]:
                 tree.relay()
 
         def rows_end(r):
+            if r == 0:
+                for copy in x_own:
+                    copy.wait()
+                for tree, dz in zip(row_state[0], (1, 0)):
+                    tree.part = lambda d, h, dz=dz: own_x.at[dz, pl.ds(64 * h, 64)]
             for h in range(2):
                 add_into(v_rows.at[r, 1, pl.ds(64 * h, 64)], row_state[r][0].close(h), 32)
             copy = sends.start(v_rows.at[r, 1], lambda: land_zb.at[r], place.group(0, 1, 0))
@@ -675,8 +730,9 @@
             for copy in own_loads[i]:
                 copy.wait()
             trees[i].part = lambda d, h: own_p.at[i, {-1: 0, 1: 1, 0: 2 + h}[d]]
-            trees[i].out = lambda h: out_y.at[i, h]
-            trees[i].relay()
+            trees[i].out = lambda h: own_p.at[i, h]
+            if i > 0:
+                trees[i].relay()
 
         def y_end(i):
             m, e = Y_FIRST[i]
@@ -699,22 +755,20 @@
             dst = grads_out.at[m, e]
             add_into(dst, [dst, land_z.at[i]], 64)
 
-        rows_start(0)
+        rows_start()
         y_relay(0)
-        rows_start(1)
+        y_relay(1)
+        r0 = rows_end(0)
         d0 = down_mid(0)
-        rows_mid(0)
-        y_relay(1)
-        rows_mid(1)
         y_relay(2)
-        r0 = rows_end(0)
+        rows_mid()
+        z0 = y_end(0)
+        y_relay(3)
         d1 = down_mid(1)
-        y_relay(3)
-        z0 = y_end(0)
+        rows_last(0, r0)
         r1 = rows_end(1)
         d0.relay()
         z1 = y_end(1)
-        rows_last(0, r0)
         d1.relay()
         z2 = y_end(2)
         rows_last(1, r1)
@@ -726,13 +780,13 @@
         z_end(2, z2)
         z_end(3, z3)
         for copy in sends.made:
-            if all(copy is not c for (r, _), c in shares.items() if r == 1):
+            if all(copy is not c for c in shares.values()):
                 copy.wait_send()
 
     def buf(*shape):
         return pltpu.VMEM(shape, BF16)
 
-    d = o_first.shape[-1]
+    d = t_first.shape[-1]
     slab = (H_ROWS, W_COLS)
     pl.run_scoped(
         first_phase,
@@ -743,8 +797,8 @@
     )
     pl.run_scoped(
         second_phase,
-        buf(4, 4, *slab), buf(4, 2, *slab), buf(4, *slab), buf(2, 4, *slab), buf(2, *slab),
-        buf(2, 8, 128, d), buf(2, 128, d), buf(2, 2, 2, 64, d), buf(2, 2, 128, d),
+        buf(4, 4, *slab), buf(4, *slab), buf(2, 4, *slab), buf(2, *slab),
+        buf(8, 128, d), buf(2, 128, d), buf(2, 128, d), buf(2, 2, 64, d), buf(2, 2, 128, d),
     )
 
 
@@ -767,7 +821,7 @@
             jax.ShapeDtypeStruct((3, 2) + slab, F32),
             jax.ShapeDtypeStruct((3, 2, H_ROWS, d), BF16),
             jax.ShapeDtypeStruct((8, 128, d), BF16),
-            jax.ShapeDtypeStruct((2, 8, 128, d), BF16),
+            jax.ShapeDtypeStruct((8, 128, d), BF16),
         ),
         in_specs=[hbm] * 8 + [vmem] * 2,
         out_specs=(vmem,) * 4 + (hbm,) * 3,
@@ -775,6 +829,7 @@
             buf(4, 3, 2, *slab), buf(4, *slab), buf(2, 3, *slab), buf(2, 4, *slab),
             buf(2, 2, 3, 2, 64, d), buf(2, 128, d),
             pltpu.VMEM((16, 8, 128), F32),
+            buf(2, 2, 64, d), buf(2, *slab),
             pltpu.SemaphoreType.DMA((n,)),
             pltpu.SemaphoreType.DMA((n,)),
             pltpu.SemaphoreType.DMA((112,)),

time: 260 us -> 233 us (0.90); the launches traced: 256 us -> 233 us
  Pallas kernels: 246 us -> 223 us
    pallas_call x1, Pallas kernels: 164 us -> 143 us  [backward(): pl.pallas_call(backward_kernel, out_shape=(jax.ShapeDtypeStruct((128, d),...]
where the time goes in v2:
time: 233 us
  Pallas kernels  223 us (96%)
  local copies, waits for them, and re-layouts  8.7 us (4%)
    pallas_call x1, Pallas kernels, backward(): pl.pallas_call(backward_kernel, out_shape=(jax.ShapeDtypeStruct((128, d),...  143 us
    pallas_call x1, Pallas kernels, forward(): pl.pallas_call(forward_kernel, out_shape=(jax.ShapeDtypeStruct((2, 512, d...  79.4 us

profile of v2, /device:TPU:1, one launch (start us, length us, event | category | flops | bytes accessed | tf_op | source)
XLA Modules:
  0.0 232.8 jit_solution(3219472054933974616)
XLA Ops:
  0.6 0.7 convert_bitcast_fusion
  1.4 0.8 scatter.9.meta
  2.1 0.0 copy-start.2
  2.1 0.6 copy-done.2
  2.7 79.4 %shard_map.127 = (bf16[2,512,2048]{2,1,0:T(8,128)(2,1)}, bf16[2,512,2048]{2,1,0:T(8,128)(2,1)}, f32[2,2,512,704]{3,2,1,0:T(8,128)}, bf16[2,704,512]{2,1,0:T(8,12...) custom-call(bf16[128,2048]{1,0:T(8,128)(2,1)} %tok.1, ...), custom_call_target="tpu_custom_call" | custom-call | tf_op jit(solution)/shard_map/pallas_call | solution.py:347
  82.1 143.3 %shard_map.128 = (bf16[128,2048]{1,0:T(8,128)(2,1)}, bf16[128,2048]{1,0:T(8,128)(2,1)}, f32[8,128]{1,0:T(8,128)}, f32[3,2,704,256]{3,2,1,0:T(8,128)}, bf16[3,2,7...) custom-call(bf16[2,512,2048]{2,1,0:T(8,128)(2,1)} %get-tuple-element.41.routed_hbm, ...), custom_call_target="tpu_custom_call" | custom-call | tf_op jit(solution)/shard_map/pallas_call | solution.py:815
  225.5 1.3 slice_bitcast_fusion.3
  226.7 0.0 copy-start.1
  226.7 0.0 copy-start
  226.7 4.5 %slice_bitcast_fusion = (f32[2,704,256]{2,1,0:T(8,128)}, f32[2,256,704]{1,2,0:T(8,128)}, f32[2,256,704]{1,2,0:T(8,128)}) fusion(f32[3,2,704,256]{3,2,1,0:T(8,128)} %get-tuple-element.51), kind=kLoop, calls=%fused_computation | loop fusion | bytes 8650752 | tf_op jit(solution)/shard_map/squeeze | solution.py:859
  231.2 0.0 copy-done.1
  231.2 0.8 copy.17
  232.0 0.0 copy-done
  232.0 0.8 copy.18
  (1 shorter events, 0.0 us)
Async XLA Ops:
  2.1 0.6 copy-start.2
  226.7 4.5 %copy-start.1 = (bf16[128,2048]{1,0:T(8,128)(2,1)S(1)}, bf16[128,2048]{1,0:T(8,128)(2,1)}, u32[]{:S(2)}) copy-start(bf16[128,2048]{1,0:T(8,128)(2,1)} %get-tuple-element.61) | copy-start | bytes 1572868
  226.7 5.3 %copy-start = (bf16[128,2048]{1,0:T(8,128)(2,1)S(1)}, bf16[128,2048]{1,0:T(8,128)(2,1)}, u32[]{:S(2)}) copy-start(bf16[128,2048]{1,0:T(8,128)(2,1)} %get-tuple-element.62) | copy-start | bytes 1572868

commit v3 on v2

--- a/solution.py
+++ b/solution.py
@@ -429,8 +429,8 @@
 
 def backward_kernel(
     routed_hbm, dy_hbm, pre_hbm, hidden_hbm, wg_hbm, wu_hbm, wd_hbm, t_first, gates_in, pick,
-    out_first, out_second, gates_out, grads_out, p_hbm, o_own, land_s,
-    land_y, land_z, land_d, land_dz, land_xb, land_zb, gates_land, early_x, early_y,
+    out_first, out_second, gates_out, grads_gate, grads_up, grads_down, p_hbm,
+    land_s, land_y, land_z, land_d, land_dz, land_xb, land_zb, gates_land, early_x, early_y,
     send_sem, recv_sem, load_sem,
 ):
     place = Place()
@@ -443,6 +443,7 @@
         return copy
 
     rows_out = (out_first, out_second)
+    grads_out = (grads_gate, grads_up, grads_down)
     sends = Sends(send_sem, recv_sem, place)
 
     def yy(d):
@@ -477,7 +478,7 @@
     row_state = {}
 
     def first_phase(
-        routed, dy, pre, hidden_t, wg, wu, wd, dhd, dg, du, dg_t, du_t, stage, o_stage
+        routed, dy, pre, hidden_t, wg, wu, wd, dhd, dg, du, dg_t, du_t, stage
     ):
         ld = [
             load(hidden_hbm, hidden_t), load(dy_hbm, dy), load(wd_hbm.at[0], wd),
@@ -573,6 +574,7 @@
                 next_wd.wait()
                 next_pre.wait()
             dhd[...] = dot_nt(dy[e], wd[...])
+            flush()
             if e == 0:
                 next_wd = load(wd_hbm.at[1], wd)
 
@@ -589,50 +591,66 @@
                 next_pre = load(pre_hbm.at[1], pre)
             dg_t[...] = dg[...].T
             du_t[...] = du[...].T
-            partial(0, e, dg_t, routed.at[e])
-            partial(1, e, du_t, routed.at[e])
-            if e == 1:
+            if e == 0:
+                partial(0, e, dg_t, routed.at[e])
+                partial(1, e, du_t, routed.at[e])
+            else:
                 for copy in next_w:
                     copy.wait()
 
-            @pl.loop(0, 4)
-            def _(n):
+            def back(n):
                 at = pl.ds(pl.multiple_of(n * 512, 512), 512)
                 total = dot_nn(dg[...], wg[:, at]) + dot_nn(du[...], wu[:, at])
-                routed[e, :, at] = total.astype(BF16)
+                dy[e, :, at] = total.astype(BF16)
+
+            pl.loop(0, 1)(back)
+            flush()
+            pl.loop(1, 4)(back)
 
             if e == 0:
+                next_w = [load(wg_hbm.at[1], wg), load(wu_hbm.at[1], wu)]
                 early_rows()
-                next_w = [load(wg_hbm.at[1], wg), load(wu_hbm.at[1], wu)]
-        for entry in pending:
-            for copy in entry[0]:
-                copy.wait()
-            open_partial(entry[1], entry[2])
-        early_partial()
 
         def back_rows(j):
             at = pl.ds(pl.multiple_of(j * 32, 32), 32)
-            rows = jnp.concatenate([routed[0, at], routed[1, at]], axis=0)
-            return dot_tn(pick[j], rows).astype(BF16)
+            rows = jnp.concatenate([dy[0, at], dy[1, at]], axis=0)
+            return dot_tn(pick[j], rows)
+
+        @pl.loop(0, 4)
+        def _(i):
+            at = pl.ds(pl.multiple_of(i * 128, 128), 128)
+            wg[at] = back_rows(i * 2 + 1).astype(BF16)
+            wu[at] = back_rows(i * 2 + 9).astype(BF16)
+
+        for i in range(8):
+            shares[i] = sends.start(
+                (wg, wu)[i // 4].at[pl.ds((i % 4) * 128, 128)], lambda i=i: land_s.at[i],
+                place.group(0, 0, 1),
+            )
+        partial(0, 1, dg_t, routed.at[1])
+        partial(1, 1, du_t, routed.at[1])
+        flush()
+        early_partial()
+        for i in range(8):
+            shares[i].wait_recv()
 
         @pl.loop(0, 8)
         def _(i):
-            at = pl.ds(pl.multiple_of(lax.rem(i, 4) * 128, 128), 128)
-            dy[i // 4, at] = back_rows(i * 2 + 1)
-
-        for i in range(8):
-            shares[i] = sends.start(
-                dy.at[i // 4, pl.ds((i % 4) * 128, 128)], lambda i=i: land_s.at[i],
-                place.group(0, 0, 1),
+            land_s[i] = (back_rows(i * 2) + land_s[i].astype(F32)).astype(BF16)
+
+        for dz in (1, 0):
+
+            def part(d, h, dz=dz):
+                return land_s.at[(d % NX) * 2 + dz, pl.ds(64 * h, 64)]
+
+            tree = Tree(
+                sends, place.group, part,
+                lambda k, h, dz=dz: land_xb.at[1, dz, k, h],
+                lambda h, part=part: part((-1, 1)[h], h),
+                32,
             )
-        outs = []
-        for i in range(8):
-            if i >= 2:
-                outs[i - 2].wait()
-            o_stage[i % 2] = back_rows(i * 2)
-            outs.append(load(o_stage.at[i % 2], o_own.at[i]))
-        for copy in outs[6:]:
-            copy.wait()
+            tree.open()
+            row_state.setdefault(1, []).append(tree)
         for i in range(8):
             shares[i].wait_send()
         for copy in gate_sends:
@@ -642,8 +660,7 @@
             total = total + gates_land[i]
         gates_out[...] = total
 
-    def second_phase(own_p, out_z, t_down, out_d, t_rows, own_x, s_stage, out_xb, v_rows):
-        own_rows = [load(o_own.at[i], t_rows.at[i]) for i in range(8)]
+    def second_phase(own_p, out_z, t_down, out_d, own_x, v_rows):
         x_own = [load(t_first.at[dz], own_x.at[dz]) for dz in range(2)]
         own_loads = {}
         for i, (m, e) in enumerate(Y_FIRST):
@@ -656,31 +673,6 @@
         down_loads = {}
         for i, (m, e) in enumerate(Z_FIRST):
             down_loads[i] = [load(p_slice(m, e, d, place.zh), t_down.at[i, d]) for d in range(NY)]
-
-        def rows_start():
-            gets = []
-            for i in range(8):
-                shares[i].wait_recv()
-            for i in range(9):
-                if i < 8:
-                    gets.append(load(land_s.at[i], s_stage.at[i % 2]))
-                if i > 0:
-                    gets[i - 1].wait()
-                    own_rows[i - 1].wait()
-                    dst = t_rows.at[i - 1]
-                    add_into(dst, [dst, s_stage.at[(i - 1) % 2]], 32)
-            made = []
-            for dz in (1, 0):
-                tree = Tree(
-                    sends, place.group,
-                    lambda d, h, dz=dz: t_rows.at[(d % NX) * 2 + dz, pl.ds(64 * h, 64)],
-                    lambda k, h, dz=dz: land_xb.at[1, dz, k, h],
-                    lambda h, dz=dz: out_xb.at[dz, h],
-                    32,
-                )
-                tree.open()
-                made.append(tree)
-            row_state[1] = made
 
         def rows_mid():
             for tree in row_state[1]:
@@ -724,7 +716,7 @@
             m, e = Z_FIRST[i]
             half = H_ROWS // 2
             for h in range(2):
-                add_into(grads_out.at[m, e, pl.ds(half * h, half)], tree.close(h), 32)
+                add_into(grads_out[m].at[e, pl.ds(half * h, half)], tree.close(h), 32)
 
         def y_relay(i):
             for copy in own_loads[i]:
@@ -745,37 +737,36 @@
 
                 @pl.when(place.zh == h)
                 def _():
-                    add_into(grads_out.at[m, e], terms, 64)
+                    add_into(grads_out[m].at[e], terms, 64)
 
             return sends.start(out_z.at[i], lambda: land_z.at[i], place.col(0, 1))
 
         def z_end(i, copy):
             m, e = Y_FIRST[i]
             copy.wait_recv()
-            dst = grads_out.at[m, e]
+            dst = grads_out[m].at[e]
             add_into(dst, [dst, land_z.at[i]], 64)
 
-        rows_start()
         y_relay(0)
         y_relay(1)
+        d0 = down_mid(0)
         r0 = rows_end(0)
-        d0 = down_mid(0)
+        z0 = y_end(0)
+        rows_mid()
+        z1 = y_end(1)
         y_relay(2)
-        rows_mid()
-        z0 = y_end(0)
         y_relay(3)
         d1 = down_mid(1)
         rows_last(0, r0)
+        d0.relay()
+        z_end(0, z0)
+        z2 = y_end(2)
         r1 = rows_end(1)
-        d0.relay()
-        z1 = y_end(1)
         d1.relay()
-        z2 = y_end(2)
+        z_end(1, z1)
+        z3 = y_end(3)
+        down_end(0, d0)
         rows_last(1, r1)
-        z_end(0, z0)
-        down_end(0, d0)
-        z3 = y_end(3)
-        z_end(1, z1)
         down_end(1, d1)
         z_end(2, z2)
         z_end(3, z3)
@@ -793,12 +784,12 @@
         buf(2, 512, d), buf(2, 512, d), pltpu.VMEM((2, 512, H_ROWS), F32), buf(2, H_ROWS, 512),
         buf(H_ROWS, d), buf(H_ROWS, d), buf(H_ROWS, d), pltpu.VMEM((512, H_ROWS), F32),
         buf(512, H_ROWS), buf(512, H_ROWS), buf(H_ROWS, 512), buf(H_ROWS, 512),
-        buf(2, H_ROWS, 1024), buf(2, 128, d),
+        buf(2, H_ROWS, 1024),
     )
     pl.run_scoped(
         second_phase,
         buf(4, 4, *slab), buf(4, *slab), buf(2, 4, *slab), buf(2, *slab),
-        buf(8, 128, d), buf(2, 128, d), buf(2, 128, d), buf(2, 2, 64, d), buf(2, 2, 128, d),
+        buf(2, 128, d), buf(2, 2, 128, d),
     )
 
 
@@ -818,15 +809,15 @@
             jax.ShapeDtypeStruct((128, d), BF16),
             jax.ShapeDtypeStruct((128, d), BF16),
             jax.ShapeDtypeStruct((8, 128), F32),
-            jax.ShapeDtypeStruct((3, 2) + slab, F32),
+            jax.ShapeDtypeStruct((2,) + slab, F32),
+            jax.ShapeDtypeStruct((2,) + slab, F32),
+            jax.ShapeDtypeStruct((2,) + slab, F32),
             jax.ShapeDtypeStruct((3, 2, H_ROWS, d), BF16),
-            jax.ShapeDtypeStruct((8, 128, d), BF16),
-            jax.ShapeDtypeStruct((8, 128, d), BF16),
         ),
         in_specs=[hbm] * 8 + [vmem] * 2,
-        out_specs=(vmem,) * 4 + (hbm,) * 3,
+        out_specs=(vmem,) * 6 + (hbm,),
         scratch_shapes=[
-            buf(4, 3, 2, *slab), buf(4, *slab), buf(2, 3, *slab), buf(2, 4, *slab),
+            buf(8, 128, d), buf(4, 3, 2, *slab), buf(4, *slab), buf(2, 3, *slab), buf(2, 4, *slab),
             buf(2, 2, 3, 2, 64, d), buf(2, 128, d),
             pltpu.VMEM((16, 8, 128), F32),
             buf(2, 2, 64, d), buf(2, *slab),
@@ -837,7 +828,7 @@
         compiler_params=pltpu.CompilerParams(
             collective_id=1, has_side_effects=True, vmem_limit_bytes=63 * 2**20
         ),
-    )(*operands)[:4]
+    )(*operands)[:6]
 
 
 def shards(tokens, cotangent, route_gates, expert_ids, slot_index, w_gate, w_up, w_down):
@@ -847,16 +838,16 @@
     routed, grad_rows, pre, hidden_t, o_out, gates_in, pick = forward(
         tokens, cotangent, meta, wg, wu, w_down
     )
-    out, grad, gates, grads = backward(
+    out, grad, gates, grad_gate, grad_up, grad_down = backward(
         routed, grad_rows, pre, hidden_t, wg, wu, w_down, o_out, gates_in, pick
     )
     return (
         out,
         grad,
         gates[0:6].T,
-        grads[0].transpose(0, 2, 1),
-        grads[1].transpose(0, 2, 1),
-        grads[2],
+        grad_gate.transpose(0, 2, 1),
+        grad_up.transpose(0, 2, 1),
+        grad_down,
     )
 
 

time: 233 us -> 235 us (level)
  local copies, waits for them, and re-layouts: 8.7 us -> 11.3 us
    unnamed x8 -> x11, local copies, waits for them, and re-layouts: 2.19 us -> 9.12 us
    squeeze x1 -> x0, local copies, waits for them, and re-layouts: 4.46 us -> none  [shards(): grads[2]]
where the time goes in v3:
time: 235 us
  Pallas kernels  222 us (94%)
  local copies, waits for them, and re-layouts  11.3 us (5%)
    pallas_call x1, Pallas kernels, backward(): pl.pallas_call(backward_kernel, out_shape=(jax.ShapeDtypeStruct((128, d),...  143 us
    pallas_call x1, Pallas kernels, forward(): pl.pallas_call(forward_kernel, out_shape=(jax.ShapeDtypeStruct((2, 512, d...  79.4 us
    unnamed x11, local copies, waits for them, and re-layouts  9.12 us

profile of v3, /device:TPU:1, one launch (start us, length us, event | category | flops | bytes accessed | tf_op | source)
XLA Modules:
  0.0 234.7 jit_solution(9715916684579276344)
XLA Ops:
  0.6 0.7 convert_bitcast_fusion
  1.3 0.8 scatter.9.meta
  2.1 0.0 copy-start.2
  2.1 0.6 copy-done.2
  2.7 79.4 %shard_map.127 = (bf16[2,512,2048]{2,1,0:T(8,128)(2,1)}, bf16[2,512,2048]{2,1,0:T(8,128)(2,1)}, f32[2,2,512,704]{3,2,1,0:T(8,128)}, bf16[2,704,512]{2,1,0:T(8,12...) custom-call(bf16[128,2048]{1,0:T(8,128)(2,1)} %tok.1, ...), custom_call_target="tpu_custom_call" | custom-call | tf_op jit(solution)/shard_map/pallas_call | solution.py:347
  82.1 142.6 %shard_map.128 = (bf16[128,2048]{1,0:T(8,128)(2,1)}, bf16[128,2048]{1,0:T(8,128)(2,1)}, f32[8,128]{1,0:T(8,128)}, f32[2,704,256]{2,1,0:T(8,128)}, f32[2,704,256]...) custom-call(bf16[2,512,2048]{2,1,0:T(8,128)(2,1)} %get-tuple-element.43.routed_hbm, ...), custom_call_target="tpu_custom_call" | custom-call | tf_op jit(solution)/shard_map/pallas_call | solution.py:806
  224.7 0.0 copy-start.1
  224.7 0.0 copy-start
  224.7 1.4 slice_bitcast_fusion
  226.2 1.9 copy.20
  228.0 1.9 copy.21
  229.9 2.6 %copy.22 = f32[2,256,704]{1,2,0:T(8,128)} copy(f32[2,256,704]{1,2,0:T(8,128)} %bitcast.14) | data formatting | bytes 2883584
  232.5 0.0 copy-done.1
  232.5 1.1 copy.23
  233.6 0.0 copy-done
  233.6 1.1 copy.24
  (1 shorter events, 0.0 us)
Async XLA Ops:
  2.1 0.6 copy-start.2
  224.7 7.8 %copy-start.1 = (f32[2,704,256]{2,1,0:T(8,128)S(1)}, f32[2,704,256]{2,1,0:T(8,128)}, u32[]{:S(2)}) copy-start(f32[2,704,256]{2,1,0:T(8,128)} %get-tuple-element.54) | copy-start | bytes 4325380
  224.7 8.9 %copy-start = (f32[2,704,256]{2,1,0:T(8,128)S(1)}, f32[2,704,256]{2,1,0:T(8,128)}, u32[]{:S(2)}) copy-start(f32[2,704,256]{2,1,0:T(8,128)} %get-tuple-element.67) | copy-start | bytes 4325380

commit v4 on v3

--- a/solution.py
+++ b/solution.py
@@ -429,8 +429,8 @@
 
 def backward_kernel(
     routed_hbm, dy_hbm, pre_hbm, hidden_hbm, wg_hbm, wu_hbm, wd_hbm, t_first, gates_in, pick,
-    out_first, out_second, gates_out, grads_gate, grads_up, grads_down, p_hbm,
-    land_s, land_y, land_z, land_d, land_dz, land_xb, land_zb, gates_land, early_x, early_y,
+    out_first, out_second, gates_out, grads_hbm, p_hbm,
+    land_s, land_y, land_z, land_d, land_dz, land_xb, land_zb, gates_land, early_x, early_y, grads,
     send_sem, recv_sem, load_sem,
 ):
     place = Place()
@@ -443,7 +443,6 @@
         return copy
 
     rows_out = (out_first, out_second)
-    grads_out = (grads_gate, grads_up, grads_down)
     sends = Sends(send_sem, recv_sem, place)
 
     def yy(d):
@@ -716,7 +715,8 @@
             m, e = Z_FIRST[i]
             half = H_ROWS // 2
             for h in range(2):
-                add_into(grads_out[m].at[e, pl.ds(half * h, half)], tree.close(h), 32)
+                add_into(grads.at[m, e, pl.ds(half * h, half)], tree.close(h), 32)
+            finals.append(load(grads.at[m, e], grads_hbm.at[m, e]))
 
         def y_relay(i):
             for copy in own_loads[i]:
@@ -737,19 +737,21 @@
 
                 @pl.when(place.zh == h)
                 def _():
-                    add_into(grads_out[m].at[e], terms, 64)
+                    add_into(grads.at[m, e], terms, 64)
 
             return sends.start(out_z.at[i], lambda: land_z.at[i], place.col(0, 1))
 
         def z_end(i, copy):
             m, e = Y_FIRST[i]
             copy.wait_recv()
-            dst = grads_out[m].at[e]
+            dst = grads.at[m, e]
             add_into(dst, [dst, land_z.at[i]], 64)
+            finals.append(load(dst, grads_hbm.at[m, e]))
 
         y_relay(0)
         y_relay(1)
         d0 = down_mid(0)
+        finals = []
         r0 = rows_end(0)
         z0 = y_end(0)
         rows_mid()
@@ -770,6 +772,8 @@
         down_end(1, d1)
         z_end(2, z2)
         z_end(3, z3)
+        for copy in finals:
+            copy.wait()
         for copy in sends.made:
             if all(copy is not c for c in shares.values()):
                 copy.wait_send()
@@ -809,18 +813,16 @@
             jax.ShapeDtypeStruct((128, d), BF16),
             jax.ShapeDtypeStruct((128, d), BF16),
             jax.ShapeDtypeStruct((8, 128), F32),
-            jax.ShapeDtypeStruct((2,) + slab, F32),
-            jax.ShapeDtypeStruct((2,) + slab, F32),
-            jax.ShapeDtypeStruct((2,) + slab, F32),
+            jax.ShapeDtypeStruct((3, 2) + slab, F32),
             jax.ShapeDtypeStruct((3, 2, H_ROWS, d), BF16),
         ),
         in_specs=[hbm] * 8 + [vmem] * 2,
-        out_specs=(vmem,) * 6 + (hbm,),
+        out_specs=(vmem,) * 3 + (hbm,) * 2,
         scratch_shapes=[
             buf(8, 128, d), buf(4, 3, 2, *slab), buf(4, *slab), buf(2, 3, *slab), buf(2, 4, *slab),
             buf(2, 2, 3, 2, 64, d), buf(2, 128, d),
             pltpu.VMEM((16, 8, 128), F32),
-            buf(2, 2, 64, d), buf(2, *slab),
+            buf(2, 2, 64, d), buf(2, *slab), pltpu.VMEM((3, 2) + slab, F32),
             pltpu.SemaphoreType.DMA((n,)),
             pltpu.SemaphoreType.DMA((n,)),
             pltpu.SemaphoreType.DMA((112,)),
@@ -828,26 +830,27 @@
         compiler_params=pltpu.CompilerParams(
             collective_id=1, has_side_effects=True, vmem_limit_bytes=63 * 2**20
         ),
-    )(*operands)[:6]
+    )(*operands)[:4]
 
 
 def shards(tokens, cotangent, route_gates, expert_ids, slot_index, w_gate, w_up, w_down):
     target = (expert_ids * 32 + slot_index).astype(F32).T
-    meta = jnp.zeros((16, 128), F32).at[0:6].set(target).at[8:14].set(route_gates.T)
+    gap = jnp.zeros((2, 128), F32)
+    meta = jnp.concatenate([target, gap, route_gates.T, gap])
     wg, wu = w_gate.transpose(0, 2, 1), w_up.transpose(0, 2, 1)
     routed, grad_rows, pre, hidden_t, o_out, gates_in, pick = forward(
         tokens, cotangent, meta, wg, wu, w_down
     )
-    out, grad, gates, grad_gate, grad_up, grad_down = backward(
+    out, grad, gates, grads = backward(
         routed, grad_rows, pre, hidden_t, wg, wu, w_down, o_out, gates_in, pick
     )
     return (
         out,
         grad,
         gates[0:6].T,
-        grad_gate.transpose(0, 2, 1),
-        grad_up.transpose(0, 2, 1),
-        grad_down,
+        grads[0].transpose(0, 2, 1),
+        grads[1].transpose(0, 2, 1),
+        grads[2],
     )
 
 

time: 235 us -> 232 us (0.987)
  local copies, waits for them, and re-layouts: 11.3 us -> 7.33 us
    unnamed x11 -> x6, local copies, waits for them, and re-layouts: 9.12 us -> 1.59 us
    squeeze x0 -> x1, local copies, waits for them, and re-layouts: none -> 4.46 us  [shards(): grads[2]]
where the time goes in v4:
time: 232 us
  Pallas kernels  222 us (96%)
  local copies, waits for them, and re-layouts  7.33 us (3%)
    pallas_call x1, Pallas kernels, backward(): pl.pallas_call(backward_kernel, out_shape=(jax.ShapeDtypeStruct((128, d),...  142 us
    pallas_call x1, Pallas kernels, forward(): pl.pallas_call(forward_kernel, out_shape=(jax.ShapeDtypeStruct((2, 512, d...  79.4 us

profile of v4, /device:TPU:1, one launch (start us, length us, event | category | flops | bytes accessed | tf_op | source)
XLA Modules:
  0.0 231.6 jit_solution(9851048729559345657)
XLA Ops:
  0.6 0.7 convert_bitcast_fusion
  1.3 1.3 pad_maximum_fusion.meta
  2.6 79.4 %shard_map.127 = (bf16[2,512,2048]{2,1,0:T(8,128)(2,1)}, bf16[2,512,2048]{2,1,0:T(8,128)(2,1)}, f32[2,2,512,704]{3,2,1,0:T(8,128)}, bf16[2,704,512]{2,1,0:T(8,12...) custom-call(bf16[128,2048]{1,0:T(8,128)(2,1)} %tok.1, ...), custom_call_target="tpu_custom_call" | custom-call | tf_op jit(solution)/shard_map/pallas_call | solution.py:347
  82.0 142.2 %shard_map.128 = (bf16[128,2048]{1,0:T(8,128)(2,1)}, bf16[128,2048]{1,0:T(8,128)(2,1)}, f32[8,128]{1,0:T(8,128)}, f32[3,2,704,256]{3,2,1,0:T(8,128)}, bf16[3,2,704,2048]{3,2,1,0:T(8,128)(2,1)}) custom-call(bf16[2,512,2048]{2,1,0:T(8,128)(2,1)} %get-tuple-element.17.routed_hbm, bf16[2,512,2048]{2,1,0:T(8,128)(2,1)} %get-tuple-element.18.dy_hbm, ...), custom_call_target="tpu_custom_call" | custom-call | tf_op jit(solution)/shard_map/pallas_call | solution.py:810
  224.2 1.3 slice_bitcast_fusion.3
  225.5 0.0 copy-start.1
  225.5 0.0 copy-start
  225.5 4.5 %slice_bitcast_fusion = (f32[2,704,256]{2,1,0:T(8,128)}, f32[2,256,704]{1,2,0:T(8,128)}, f32[2,256,704]{1,2,0:T(8,128)}) fusion(f32[3,2,704,256]{3,2,1,0:T(8,128)} %get-tuple-element.27), kind=kLoop, calls=%fused_computation | loop fusion | bytes 8650752 | tf_op jit(solution)/shard_map/squeeze | solution.py:853
  230.0 0.0 copy-done.1
  230.0 0.8 copy.16
  230.8 0.0 copy-done
  230.8 0.8 copy.17
  (1 shorter events, 0.0 us)
Async XLA Ops:
  225.5 4.5 %copy-start.1 = (bf16[128,2048]{1,0:T(8,128)(2,1)S(1)}, bf16[128,2048]{1,0:T(8,128)(2,1)}, u32[]{:S(2)}) copy-start(bf16[128,2048]{1,0:T(8,128)(2,1)} %get-tuple-element.37) | copy-start | bytes 1572868
  225.5 5.3 %copy-start = (bf16[128,2048]{1,0:T(8,128)(2,1)S(1)}, bf16[128,2048]{1,0:T(8,128)(2,1)}, u32[]{:S(2)}) copy-start(bf16[128,2048]{1,0:T(8,128)(2,1)} %get-tuple-element.38) | copy-start | bytes 1572868

commit v5 on v4

--- a/solution.py
+++ b/solution.py
@@ -182,14 +182,17 @@
 
 
 def forward_kernel(
-    tok, cot, meta, wg_hbm, wu_hbm, wd_hbm,
+    tok, cot, ids, slots, route, wg_hbm, wu_hbm, wd_hbm,
     routed_o, dy_o, pre_o, hidden_o, totals_o, gates_o, pick,
-    tok_all, cot_all, meta_all, wg, wu, wd, routed, y_rows, dy, pre, hidden, hidden_t, gate_col, land_s,
+    tok_all, cot_all, meta_all, wg, wu, wd, routed, y_rows, dy, pre, hidden, hidden_t, gate_col, land_s, meta,
     send_sem, recv_sem, copy_sem,
 ):
     place = Place()
     enter([place.group(*r) for r in GROUP[1:]])
     copies = []
+    meta[...] = jnp.zeros((16, 128), F32)
+    meta[0:6] = (ids[...] * 32 + slots[...]).astype(F32)
+    meta[8:14] = route[...]
 
     def local(src, dst):
         copy = pltpu.make_async_copy(src, dst, copy_sem.at[len(copies)])
@@ -340,7 +343,7 @@
     sends.drain()
 
 
-def forward(tok, cot, meta, w_gate, w_up, w_down):
+def forward(tok, cot, ids, slots, route, w_gate, w_up, w_down):
     d = tok.shape[1]
     hbm = pl.BlockSpec(memory_space=pl.ANY)
     vmem = pl.BlockSpec(memory_space=pltpu.VMEM)
@@ -355,12 +358,12 @@
             jax.ShapeDtypeStruct((16, 8, 128), F32),
             jax.ShapeDtypeStruct((16, 64, 128), BF16),
         ),
-        in_specs=[hbm] * 6,
+        in_specs=[hbm] * 2 + [vmem] * 3 + [hbm] * 3,
         out_specs=(hbm, hbm, hbm, hbm, hbm, vmem, vmem),
         scratch_shapes=[
             pltpu.VMEM((16, 128, d), BF16),
             pltpu.VMEM((16, 128, d), BF16),
-            pltpu.VMEM((16,) + meta.shape, F32),
+            pltpu.VMEM((16, 16, 128), F32),
             pltpu.VMEM(w_gate.shape, BF16),
             pltpu.VMEM(w_up.shape, BF16),
             pltpu.VMEM(w_down.shape, BF16),
@@ -372,6 +375,7 @@
             pltpu.VMEM((2, H_ROWS, 512), BF16),
             pltpu.VMEM((16, 64, 128), F32),
             pltpu.VMEM((8, 128, d), BF16),
+            pltpu.VMEM((16, 128), F32),
             pltpu.SemaphoreType.DMA((128,)),
             pltpu.SemaphoreType.DMA((128,)),
             pltpu.SemaphoreType.DMA((32,)),
@@ -379,7 +383,7 @@
         compiler_params=pltpu.CompilerParams(
             collective_id=0, has_side_effects=True, vmem_limit_bytes=63 * 2**20
         ),
-    )(tok, cot, meta, w_gate, w_up, w_down)
+    )(tok, cot, ids, slots, route, w_gate, w_up, w_down)
 
 
 def add_into(dst, terms, chunk):
@@ -834,12 +838,9 @@
 
 
 def shards(tokens, cotangent, route_gates, expert_ids, slot_index, w_gate, w_up, w_down):
-    target = (expert_ids * 32 + slot_index).astype(F32).T
-    gap = jnp.zeros((2, 128), F32)
-    meta = jnp.concatenate([target, gap, route_gates.T, gap])
     wg, wu = w_gate.transpose(0, 2, 1), w_up.transpose(0, 2, 1)
     routed, grad_rows, pre, hidden_t, o_out, gates_in, pick = forward(
-        tokens, cotangent, meta, wg, wu, w_down
+        tokens, cotangent, expert_ids.T, slot_index.T, route_gates.T, wg, wu, w_down
     )
     out, grad, gates, grads = backward(
         routed, grad_rows, pre, hidden_t, wg, wu, w_down, o_out, gates_in, pick

time: 232 us -> 230 us (level)
  no operation moved by 1% of the time
where the time goes in v5:
time: 230 us
  Pallas kernels  222 us (97%)
  local copies, waits for them, and re-layouts  7.33 us (3%)
    pallas_call x1, Pallas kernels, backward(): pl.pallas_call(backward_kernel, out_shape=(jax.ShapeDtypeStruct((128, d),...  142 us
    pallas_call x1, Pallas kernels, forward(): pl.pallas_call(forward_kernel, out_shape=(jax.ShapeDtypeStruct((2, 512, d...  79.8 us

profile of v5, /device:TPU:1, one launch (start us, length us, event | category | flops | bytes accessed | tf_op | source)
XLA Modules:
  0.0 229.5 jit_solution(3194094562723771944)
XLA Ops:
  0.6 79.8 %shard_map.127 = (bf16[2,512,2048]{2,1,0:T(8,128)(2,1)}, bf16[2,512,2048]{2,1,0:T(8,128)(2,1)}, f32[2,2,512,704]{3,2,1,0:T(8,128)}, bf16[2,704,512]{2,1,0:T(8,12...) custom-call(bf16[128,2048]{1,0:T(8,128)(2,1)} %tok.1, ...), custom_call_target="tpu_custom_call" | custom-call | tf_op jit(solution)/shard_map/pallas_call | solution.py:350
  80.4 141.8 %shard_map.128 = (bf16[128,2048]{1,0:T(8,128)(2,1)}, bf16[128,2048]{1,0:T(8,128)(2,1)}, f32[8,128]{1,0:T(8,128)}, f32[3,2,704,256]{3,2,1,0:T(8,128)}, bf16[3,2,704,2048]{3,2,1,0:T(8,128)(2,1)}) custom-call(bf16[2,512,2048]{2,1,0:T(8,128)(2,1)} %get-tuple-element.17.routed_hbm, bf16[2,512,2048]{2,1,0:T(8,128)(2,1)} %get-tuple-element.18.dy_hbm, ...), custom_call_target="tpu_custom_call" | custom-call | tf_op jit(solution)/shard_map/pallas_call | solution.py:814
  222.2 1.3 slice_bitcast_fusion.3
  223.5 0.0 copy-start.1
  223.5 0.0 copy-start
  223.5 4.5 %slice_bitcast_fusion = (f32[2,704,256]{2,1,0:T(8,128)}, f32[2,256,704]{1,2,0:T(8,128)}, f32[2,256,704]{1,2,0:T(8,128)}) fusion(f32[3,2,704,256]{3,2,1,0:T(8,128)} %get-tuple-element.27), kind=kLoop, calls=%fused_computation | loop fusion | bytes 8650752 | tf_op jit(solution)/shard_map/squeeze | solution.py:854
  227.9 0.0 copy-done.1
  227.9 0.8 copy.16
  228.7 0.0 copy-done
  228.7 0.8 copy.17
Async XLA Ops:
  223.5 4.5 %copy-start.1 = (bf16[128,2048]{1,0:T(8,128)(2,1)S(1)}, bf16[128,2048]{1,0:T(8,128)(2,1)}, u32[]{:S(2)}) copy-start(bf16[128,2048]{1,0:T(8,128)(2,1)} %get-tuple-element.37) | copy-start | bytes 1572868
  223.5 5.3 %copy-start = (bf16[128,2048]{1,0:T(8,128)(2,1)S(1)}, bf16[128,2048]{1,0:T(8,128)(2,1)}, u32[]{:S(2)}) copy-start(bf16[128,2048]{1,0:T(8,128)(2,1)} %get-tuple-element.38) | copy-start | bytes 1572868
